TPU v7x, 128 devices: a whole 4x4x4 slice. The times are simulated.
128 devices in a mesh: row: 8 (over x_hi, z), col: 16 (over y, x_lo, core).
Axes of the slice: x: 4 (x_hi: 2, x_lo: 2; x = x_hi * 2 + x_lo), y: 4, z: 4, core: 2. Of those that a mesh axis runs over, the one named last changes fastest.
Arguments:
- a_blocks: float32 [2560, 64, 64], P(('row', 'col')), may hold values from -0.75 to 0.75
- a_rows: int32 [2560], P(('row', 'col')), may hold values from 0 to 15, as said below
- a_cols: int32 [2560], P(('row', 'col')), may hold values from 0 to 1023, as said below
- a_keep: int32 [2560], P(('row', 'col')), may hold values 0 or 1
- b_blocks: float32 [8192, 64, 64], P(('row', 'col')), may hold values from -0.75 to 0.75
- b_rows: int32 [8192], P(('row', 'col')), may hold values from 0 to 1023, as said below
- b_cols: int32 [8192], P(('row', 'col')), may hold values from 0 to 127, as said below
Outputs:
- c_panel: float32 [1024, 8192], P('row', 'col')
Inputs may be any that keep to these rules, and one draw needn't show every extreme that they name: `a_rows`: the stored left blocks are laid out in 8 x 16 runs of 20, run d = r * 16 + c; run d holds blocks of block rows r * 2 to r * 2 + 1 only, no position twice. `a_cols`: run d = r * 16 + c of the left blocks has inner block indices c * 64 to c * 64 + 63 only. `b_rows`: the stored right blocks are laid out in runs of 64, run d = r * 16 + c; its first 32 blocks have inner block indices in group r (r * 64 to r * 64 + 63), the last 32 in group r + 8; no position twice. `b_cols`: run d = r * 16 + c of the right blocks has block columns c * 8 to c * 8 + 7 only.
All inputs are finite; a program needn't handle non-finite values. No bound on the sum of `a_keep` on one device may be relied on, other than what follows from the above.
Results may differ from a plain program's by a relative error of at most 0.0003.
Values sent between devices are 32-bit elements; how exact they have to be, the bound alone decides.
A program may use at most 192 MiB of HBM per device.

v0:
```python
import jax
import jax.numpy as jnp
from jax import lax
from jax.sharding import PartitionSpec as P

NB = 1024
RW = 2
CW = 8


def from_behind(value, axis, steps):
    count = lax.axis_size(axis)
    pairs = [(source, (source + steps) % count) for source in range(count)]
    return lax.ppermute(value, axis, pairs)


def dense_left(left_part, row_first, k_first, group_span):
    left_blk, left_row, left_col, left_mask = left_part
    block_size = left_blk.shape[1]
    scaled = left_blk * left_mask.astype(jnp.float32)[:, None, None]
    panel = jnp.zeros((RW, block_size, group_span, block_size), jnp.float32)
    panel = panel.at[left_row - row_first, :, left_col - k_first, :].add(scaled)
    return panel.reshape(RW * block_size, group_span * block_size)


def product_panel(left_dense, right_part, col_first, k_first, group_span):
    right_blk, right_row, right_col = right_part
    block_size = right_blk.shape[1]
    dense_b = jnp.zeros((group_span, block_size, CW, block_size), jnp.float32)
    dense_b = dense_b.at[right_row - k_first, :, right_col - col_first, :].add(right_blk)
    dense_b = dense_b.reshape(group_span * block_size, CW * block_size)
    return jnp.dot(
        left_dense, dense_b, precision=lax.Precision.HIGHEST, preferred_element_type=jnp.float32
    )


def regroup(member, n_row, n_col, half_slots):
    tail_shape = member.shape[1:]
    split = member.reshape((n_row, 2, half_slots) + tail_shape)
    return jnp.swapaxes(split, 0, 1).reshape((n_col, half_slots) + tail_shape)


def on_device(a_blocks, a_rows, a_cols, a_keep, b_blocks, b_rows, b_cols):
    n_row = lax.axis_size("row")
    n_col = lax.axis_size("col")
    group_span = NB // n_col
    half_slots = b_blocks.shape[0] // 2
    row_index = lax.axis_index("row")
    col_index = lax.axis_index("col")
    row_first = row_index * RW
    gathered = (
        lax.all_gather(b_blocks, "row", axis=0, tiled=True),
        lax.all_gather(b_rows, "row", axis=0, tiled=True),
        lax.all_gather(b_cols, "row", axis=0, tiled=True),
    )
    by_group = tuple((regroup(member, n_row, n_col, half_slots) for member in gathered))
    own_left = (a_blocks, a_rows, a_cols, a_keep)
    col_first = col_index * CW

    def group_right(k_group):
        return tuple(
            (lax.dynamic_index_in_dim(member, k_group, 0, keepdims=False) for member in by_group)
        )

    def turn_product(moving, k_group):
        k_first = k_group * group_span
        left_dense = dense_left(moving, row_first, k_first, group_span)
        return product_panel(left_dense, group_right(k_group), col_first, k_first, group_span)

    def cycle_turn(turn_index, carried):
        moving, accum_c = carried
        k_group = (col_index - turn_index) % n_col
        accum_c = accum_c + turn_product(moving, k_group)
        moving = from_behind((moving[0], moving[1], moving[2], moving[3]), "col", 1)
        return (moving, accum_c)

    start_c = jnp.zeros((RW * a_blocks.shape[1], CW * a_blocks.shape[1]), jnp.float32)
    moving, accum_c = lax.fori_loop(0, n_col - 1, cycle_turn, (own_left, start_c))
    last_group = (col_index - (n_col - 1)) % n_col
    result = accum_c + turn_product(moving, last_group)
    return result


def solution(mesh):
    in_specs = (
        P(("row", "col"), None, None),
        P(("row", "col")),
        P(("row", "col")),
        P(("row", "col")),
        P(("row", "col"), None, None),
        P(("row", "col")),
        P(("row", "col")),
    )
    out_specs = P("row", "col")
    return jax.shard_map(
        on_device, mesh=mesh, in_specs=in_specs, out_specs=out_specs, check_vma=False
    )
```

profile of v0, /device:TPU:0, one launch (start us, length us, event | category | flops | bytes accessed | tf_op | source)
XLA Modules:
  0.0 1472.0 jit_solution(4437717717785068679)
XLA Ops:
  12.2 14.4 all-reduce.2
  27.3 167.8 %all-gather.2.cloned.1.call-done = f32[512,64,64]{2,1,0:T(8,128)} async-done(((f32[64,64,64]{2,1,0:T(8,128)}), f32[512,64,64]{2,1,0:T(8,128)}) %all-gather.2.cloned.1.call-update) | async-done | bytes 8388624 | tf_op jit(solution)/shard_map/all_gather | solution.py:52
  207.8 1183.4 %while.24 = (s32[]{:T(128)}, f32[20,64,64]{2,1,0:T(8,128)}, s32[20]{0:T(128)S(1)}, s32[20]{0:T(128)S(1)}, s32[20]{0:T(128)S(1)}, /*index=5*/f32[128,512]{1,0:T(8...) while((s32[]{:T(128)}, f32[20,64,64]{2,1,0:T(8,128)}, ...), condition=%wide.region_3.4_spmd.clone, body=%wide.region_0.3_spmd.clone.sunk | while | flops 3221652480 | bytes 69668016 | solution.py:78
  233.2 7.9 broadcast.401
  246.2 20.1 %copy.33 = f32[64,64,8,64]{3,2,1,0:T(8,128)} copy(f32[64,64,8,64]{3,1,2,0:T(8,128)} %scatter_fusion.1) | data formatting | bytes 16777216 | tf_op jit(solution)/shard_map/while/body/eval_jaxpr/scatter-add | solution.py:30
  266.3 14.2 reshape.202
  312.4 7.9 broadcast.401
  325.3 20.1 %copy.33 = f32[64,64,8,64]{3,2,1,0:T(8,128)} copy(f32[64,64,8,64]{3,1,2,0:T(8,128)} %scatter_fusion.1) | data formatting | bytes 16777216 | tf_op jit(solution)/shard_map/while/body/eval_jaxpr/scatter-add | solution.py:30
  345.4 14.2 reshape.202
  391.2 7.9 broadcast.401
  404.2 20.1 %copy.33 = f32[64,64,8,64]{3,2,1,0:T(8,128)} copy(f32[64,64,8,64]{3,1,2,0:T(8,128)} %scatter_fusion.1) | data formatting | bytes 16777216 | tf_op jit(solution)/shard_map/while/body/eval_jaxpr/scatter-add | solution.py:30
  424.3 14.2 reshape.202
  469.4 7.9 broadcast.401
  482.4 20.1 %copy.33 = f32[64,64,8,64]{3,2,1,0:T(8,128)} copy(f32[64,64,8,64]{3,1,2,0:T(8,128)} %scatter_fusion.1) | data formatting | bytes 16777216 | tf_op jit(solution)/shard_map/while/body/eval_jaxpr/scatter-add | solution.py:30
  502.5 14.2 reshape.202
  548.6 7.9 broadcast.401
  561.5 20.1 %copy.33 = f32[64,64,8,64]{3,2,1,0:T(8,128)} copy(f32[64,64,8,64]{3,1,2,0:T(8,128)} %scatter_fusion.1) | data formatting | bytes 16777216 | tf_op jit(solution)/shard_map/while/body/eval_jaxpr/scatter-add | solution.py:30
  581.6 14.2 reshape.202
  627.7 7.9 broadcast.401
  640.6 20.1 %copy.33 = f32[64,64,8,64]{3,2,1,0:T(8,128)} copy(f32[64,64,8,64]{3,1,2,0:T(8,128)} %scatter_fusion.1) | data formatting | bytes 16777216 | tf_op jit(solution)/shard_map/while/body/eval_jaxpr/scatter-add | solution.py:30
  660.7 14.2 reshape.202
  706.5 7.9 broadcast.401
  719.5 20.1 %copy.33 = f32[64,64,8,64]{3,2,1,0:T(8,128)} copy(f32[64,64,8,64]{3,1,2,0:T(8,128)} %scatter_fusion.1) | data formatting | bytes 16777216 | tf_op jit(solution)/shard_map/while/body/eval_jaxpr/scatter-add | solution.py:30
  739.6 14.2 reshape.202
  797.7 20.1 %copy.33 = f32[64,64,8,64]{3,2,1,0:T(8,128)} copy(f32[64,64,8,64]{3,1,2,0:T(8,128)} %scatter_fusion.1) | data formatting | bytes 16777216 | tf_op jit(solution)/shard_map/while/body/eval_jaxpr/scatter-add | solution.py:30
  817.8 14.2 reshape.202
  863.9 7.9 broadcast.401
  876.8 20.1 %copy.33 = f32[64,64,8,64]{3,2,1,0:T(8,128)} copy(f32[64,64,8,64]{3,1,2,0:T(8,128)} %scatter_fusion.1) | data formatting | bytes 16777216 | tf_op jit(solution)/shard_map/while/body/eval_jaxpr/scatter-add | solution.py:30
  896.9 14.2 reshape.202
  955.9 20.1 %copy.33 = f32[64,64,8,64]{3,2,1,0:T(8,128)} copy(f32[64,64,8,64]{3,1,2,0:T(8,128)} %scatter_fusion.1) | data formatting | bytes 16777216 | tf_op jit(solution)/shard_map/while/body/eval_jaxpr/scatter-add | solution.py:30
  976.0 14.2 reshape.202
  1034.8 20.1 %copy.33 = f32[64,64,8,64]{3,2,1,0:T(8,128)} copy(f32[64,64,8,64]{3,1,2,0:T(8,128)} %scatter_fusion.1) | data formatting | bytes 16777216 | tf_op jit(solution)/shard_map/while/body/eval_jaxpr/scatter-add | solution.py:30
  1054.9 14.2 reshape.202
  1100.1 7.9 broadcast.401
  1113.1 20.1 %copy.33 = f32[64,64,8,64]{3,2,1,0:T(8,128)} copy(f32[64,64,8,64]{3,1,2,0:T(8,128)} %scatter_fusion.1) | data formatting | bytes 16777216 | tf_op jit(solution)/shard_map/while/body/eval_jaxpr/scatter-add | solution.py:30
  1133.2 14.2 reshape.202
  1179.3 7.9 broadcast.401
  1192.2 20.1 %copy.33 = f32[64,64,8,64]{3,2,1,0:T(8,128)} copy(f32[64,64,8,64]{3,1,2,0:T(8,128)} %scatter_fusion.1) | data formatting | bytes 16777216 | tf_op jit(solution)/shard_map/while/body/eval_jaxpr/scatter-add | solution.py:30
  1212.3 14.2 reshape.202
  1258.3 7.9 broadcast.401
  1271.3 20.1 %copy.33 = f32[64,64,8,64]{3,2,1,0:T(8,128)} copy(f32[64,64,8,64]{3,1,2,0:T(8,128)} %scatter_fusion.1) | data formatting | bytes 16777216 | tf_op jit(solution)/shard_map/while/body/eval_jaxpr/scatter-add | solution.py:30
  1291.4 14.2 reshape.202
  1337.3 7.9 broadcast.401
  1350.2 20.1 %copy.33 = f32[64,64,8,64]{3,2,1,0:T(8,128)} copy(f32[64,64,8,64]{3,1,2,0:T(8,128)} %scatter_fusion.1) | data formatting | bytes 16777216 | tf_op jit(solution)/shard_map/while/body/eval_jaxpr/scatter-add | solution.py:30
  1370.3 14.2 reshape.202
  1410.1 7.9 broadcast.219
  1423.1 20.1 %copy.27 = f32[64,64,8,64]{3,2,1,0:T(8,128)} copy(f32[64,64,8,64]{3,1,2,0:T(8,128)} %scatter_fusion.3) | data formatting | bytes 16777216 | tf_op jit(solution)/shard_map/scatter-add | solution.py:30
  1443.2 14.2 reshape.147
  (384 shorter events, 623.0 us)
Async XLA Ops:
  6.5 188.6 %all-gather.2.cloned.1.call-start = ((), (), s32[]{:S(2)}) async-start(), calls=%async_computation | async-start | bytes 18874368 | tf_op jit(solution)/shard_map/all_gather | solution.py:52
  209.8 77.2 %collective-permute-start = (f32[20,64,64]{2,1,0:T(8,128)}, f32[20,64,64]{2,1,0:T(8,128)}, u32[]{:S(2)}, u32[]{:S(2)}) collective-permute-start(f32[20,64,64]{2,1,0:T(8,128)} %copy.45), channel_id=1, source_target_pairs={{0,1},{1,2},{2,3},{3,4},{4,5},{5,6},{6,7},{7,8},{8,9},{9,10},{10,1... | collective-permute-start | bytes 983048 | tf_op jit(solution)/shard_map/while/body/eval_jaxpr/ppermute | solution.py:14
  209.8 77.1 %collective-permute-start.1 = (s32[20]{0:T(128)S(1)}, s32[20]{0:T(128)S(1)}, u32[]{:S(2)}, u32[]{:S(2)}) collective-permute-start(s32[20]{0:T(128)S(1)} %copy.46), channel_id=1, source_target_pairs={{0,1},{1,2},{2,3},{3,4},{4,5},{5,6},{6,7},{7,8},{8,9},{9,10},{10,1... | collective-permute-start | bytes 248 | tf_op jit(solution)/shard_map/while/body/eval_jaxpr/ppermute | solution.py:14
  210.5 76.4 %collective-permute-start.2 = (s32[20]{0:T(128)S(1)}, s32[20]{0:T(128)S(1)}, u32[]{:S(2)}, u32[]{:S(2)}) collective-permute-start(s32[20]{0:T(128)S(1)} %copy.47), channel_id=1, source_target_pairs={{0,1},{1,2},{2,3},{3,4},{4,5},{5,6},{6,7},{7,8},{8,9},{9,10},{10,1... | collective-permute-start | bytes 248 | tf_op jit(solution)/shard_map/while/body/eval_jaxpr/ppermute | solution.py:14
  210.5 76.4 %collective-permute-start.3 = (s32[20]{0:T(128)S(1)}, s32[20]{0:T(128)S(1)}, u32[]{:S(2)}, u32[]{:S(2)}) collective-permute-start(s32[20]{0:T(128)S(1)} %copy.48), channel_id=1, source_target_pairs={{0,1},{1,2},{2,3},{3,4},{4,5},{5,6},{6,7},{7,8},{8,9},{9,10},{10,1... | collective-permute-start | bytes 248 | tf_op jit(solution)/shard_map/while/body/eval_jaxpr/ppermute | solution.py:14
  289.0 77.1 %collective-permute-start = (f32[20,64,64]{2,1,0:T(8,128)}, f32[20,64,64]{2,1,0:T(8,128)}, u32[]{:S(2)}, u32[]{:S(2)}) collective-permute-start(f32[20,64,64]{2,1,0:T(8,128)} %copy.45), channel_id=1, source_target_pairs={{0,1},{1,2},{2,3},{3,4},{4,5},{5,6},{6,7},{7,8},{8,9},{9,10},{10,1... | collective-permute-start | bytes 983048 | tf_op jit(solution)/shard_map/while/body/eval_jaxpr/ppermute | solution.py:14
  289.0 77.0 %collective-permute-start.1 = (s32[20]{0:T(128)S(1)}, s32[20]{0:T(128)S(1)}, u32[]{:S(2)}, u32[]{:S(2)}) collective-permute-start(s32[20]{0:T(128)S(1)} %copy.46), channel_id=1, source_target_pairs={{0,1},{1,2},{2,3},{3,4},{4,5},{5,6},{6,7},{7,8},{8,9},{9,10},{10,1... | collective-permute-start | bytes 248 | tf_op jit(solution)/shard_map/while/body/eval_jaxpr/ppermute | solution.py:14
  289.7 76.4 %collective-permute-start.2 = (s32[20]{0:T(128)S(1)}, s32[20]{0:T(128)S(1)}, u32[]{:S(2)}, u32[]{:S(2)}) collective-permute-start(s32[20]{0:T(128)S(1)} %copy.47), channel_id=1, source_target_pairs={{0,1},{1,2},{2,3},{3,4},{4,5},{5,6},{6,7},{7,8},{8,9},{9,10},{10,1... | collective-permute-start | bytes 248 | tf_op jit(solution)/shard_map/while/body/eval_jaxpr/ppermute | solution.py:14
  289.7 76.3 %collective-permute-start.3 = (s32[20]{0:T(128)S(1)}, s32[20]{0:T(128)S(1)}, u32[]{:S(2)}, u32[]{:S(2)}) collective-permute-start(s32[20]{0:T(128)S(1)} %copy.48), channel_id=1, source_target_pairs={{0,1},{1,2},{2,3},{3,4},{4,5},{5,6},{6,7},{7,8},{8,9},{9,10},{10,1... | collective-permute-start | bytes 248 | tf_op jit(solution)/shard_map/while/body/eval_jaxpr/ppermute | solution.py:14
  368.1 76.8 %collective-permute-start = (f32[20,64,64]{2,1,0:T(8,128)}, f32[20,64,64]{2,1,0:T(8,128)}, u32[]{:S(2)}, u32[]{:S(2)}) collective-permute-start(f32[20,64,64]{2,1,0:T(8,128)} %copy.45), channel_id=1, source_target_pairs={{0,1},{1,2},{2,3},{3,4},{4,5},{5,6},{6,7},{7,8},{8,9},{9,10},{10,1... | collective-permute-start | bytes 983048 | tf_op jit(solution)/shard_map/while/body/eval_jaxpr/ppermute | solution.py:14
  368.2 76.7 %collective-permute-start.1 = (s32[20]{0:T(128)S(1)}, s32[20]{0:T(128)S(1)}, u32[]{:S(2)}, u32[]{:S(2)}) collective-permute-start(s32[20]{0:T(128)S(1)} %copy.46), channel_id=1, source_target_pairs={{0,1},{1,2},{2,3},{3,4},{4,5},{5,6},{6,7},{7,8},{8,9},{9,10},{10,1... | collective-permute-start | bytes 248 | tf_op jit(solution)/shard_map/while/body/eval_jaxpr/ppermute | solution.py:14
  368.8 76.1 %collective-permute-start.2 = (s32[20]{0:T(128)S(1)}, s32[20]{0:T(128)S(1)}, u32[]{:S(2)}, u32[]{:S(2)}) collective-permute-start(s32[20]{0:T(128)S(1)} %copy.47), channel_id=1, source_target_pairs={{0,1},{1,2},{2,3},{3,4},{4,5},{5,6},{6,7},{7,8},{8,9},{9,10},{10,1... | collective-permute-start | bytes 248 | tf_op jit(solution)/shard_map/while/body/eval_jaxpr/ppermute | solution.py:14
  368.9 76.1 %collective-permute-start.3 = (s32[20]{0:T(128)S(1)}, s32[20]{0:T(128)S(1)}, u32[]{:S(2)}, u32[]{:S(2)}) collective-permute-start(s32[20]{0:T(128)S(1)} %copy.48), channel_id=1, source_target_pairs={{0,1},{1,2},{2,3},{3,4},{4,5},{5,6},{6,7},{7,8},{8,9},{9,10},{10,1... | collective-permute-start | bytes 248 | tf_op jit(solution)/shard_map/while/body/eval_jaxpr/ppermute | solution.py:14
  447.0 76.2 %collective-permute-start = (f32[20,64,64]{2,1,0:T(8,128)}, f32[20,64,64]{2,1,0:T(8,128)}, u32[]{:S(2)}, u32[]{:S(2)}) collective-permute-start(f32[20,64,64]{2,1,0:T(8,128)} %copy.45), channel_id=1, source_target_pairs={{0,1},{1,2},{2,3},{3,4},{4,5},{5,6},{6,7},{7,8},{8,9},{9,10},{10,1... | collective-permute-start | bytes 983048 | tf_op jit(solution)/shard_map/while/body/eval_jaxpr/ppermute | solution.py:14
  447.0 76.1 %collective-permute-start.1 = (s32[20]{0:T(128)S(1)}, s32[20]{0:T(128)S(1)}, u32[]{:S(2)}, u32[]{:S(2)}) collective-permute-start(s32[20]{0:T(128)S(1)} %copy.46), channel_id=1, source_target_pairs={{0,1},{1,2},{2,3},{3,4},{4,5},{5,6},{6,7},{7,8},{8,9},{9,10},{10,1... | collective-permute-start | bytes 248 | tf_op jit(solution)/shard_map/while/body/eval_jaxpr/ppermute | solution.py:14
  525.2 77.1 %collective-permute-start = (f32[20,64,64]{2,1,0:T(8,128)}, f32[20,64,64]{2,1,0:T(8,128)}, u32[]{:S(2)}, u32[]{:S(2)}) collective-permute-start(f32[20,64,64]{2,1,0:T(8,128)} %copy.45), channel_id=1, source_target_pairs={{0,1},{1,2},{2,3},{3,4},{4,5},{5,6},{6,7},{7,8},{8,9},{9,10},{10,1... | collective-permute-start | bytes 983048 | tf_op jit(solution)/shard_map/while/body/eval_jaxpr/ppermute | solution.py:14
  525.3 77.0 %collective-permute-start.1 = (s32[20]{0:T(128)S(1)}, s32[20]{0:T(128)S(1)}, u32[]{:S(2)}, u32[]{:S(2)}) collective-permute-start(s32[20]{0:T(128)S(1)} %copy.46), channel_id=1, source_target_pairs={{0,1},{1,2},{2,3},{3,4},{4,5},{5,6},{6,7},{7,8},{8,9},{9,10},{10,1... | collective-permute-start | bytes 248 | tf_op jit(solution)/shard_map/while/body/eval_jaxpr/ppermute | solution.py:14
  525.8 76.4 %collective-permute-start.2 = (s32[20]{0:T(128)S(1)}, s32[20]{0:T(128)S(1)}, u32[]{:S(2)}, u32[]{:S(2)}) collective-permute-start(s32[20]{0:T(128)S(1)} %copy.47), channel_id=1, source_target_pairs={{0,1},{1,2},{2,3},{3,4},{4,5},{5,6},{6,7},{7,8},{8,9},{9,10},{10,1... | collective-permute-start | bytes 248 | tf_op jit(solution)/shard_map/while/body/eval_jaxpr/ppermute | solution.py:14
  526.0 76.3 %collective-permute-start.3 = (s32[20]{0:T(128)S(1)}, s32[20]{0:T(128)S(1)}, u32[]{:S(2)}, u32[]{:S(2)}) collective-permute-start(s32[20]{0:T(128)S(1)} %copy.48), channel_id=1, source_target_pairs={{0,1},{1,2},{2,3},{3,4},{4,5},{5,6},{6,7},{7,8},{8,9},{9,10},{10,1... | collective-permute-start | bytes 248 | tf_op jit(solution)/shard_map/while/body/eval_jaxpr/ppermute | solution.py:14
  604.3 77.1 %collective-permute-start = (f32[20,64,64]{2,1,0:T(8,128)}, f32[20,64,64]{2,1,0:T(8,128)}, u32[]{:S(2)}, u32[]{:S(2)}) collective-permute-start(f32[20,64,64]{2,1,0:T(8,128)} %copy.45), channel_id=1, source_target_pairs={{0,1},{1,2},{2,3},{3,4},{4,5},{5,6},{6,7},{7,8},{8,9},{9,10},{10,1... | collective-permute-start | bytes 983048 | tf_op jit(solution)/shard_map/while/body/eval_jaxpr/ppermute | solution.py:14
  604.4 77.0 %collective-permute-start.1 = (s32[20]{0:T(128)S(1)}, s32[20]{0:T(128)S(1)}, u32[]{:S(2)}, u32[]{:S(2)}) collective-permute-start(s32[20]{0:T(128)S(1)} %copy.46), channel_id=1, source_target_pairs={{0,1},{1,2},{2,3},{3,4},{4,5},{5,6},{6,7},{7,8},{8,9},{9,10},{10,1... | collective-permute-start | bytes 248 | tf_op jit(solution)/shard_map/while/body/eval_jaxpr/ppermute | solution.py:14
  605.0 76.3 %collective-permute-start.2 = (s32[20]{0:T(128)S(1)}, s32[20]{0:T(128)S(1)}, u32[]{:S(2)}, u32[]{:S(2)}) collective-permute-start(s32[20]{0:T(128)S(1)} %copy.47), channel_id=1, source_target_pairs={{0,1},{1,2},{2,3},{3,4},{4,5},{5,6},{6,7},{7,8},{8,9},{9,10},{10,1... | collective-permute-start | bytes 248 | tf_op jit(solution)/shard_map/while/body/eval_jaxpr/ppermute | solution.py:14
  605.1 76.3 %collective-permute-start.3 = (s32[20]{0:T(128)S(1)}, s32[20]{0:T(128)S(1)}, u32[]{:S(2)}, u32[]{:S(2)}) collective-permute-start(s32[20]{0:T(128)S(1)} %copy.48), channel_id=1, source_target_pairs={{0,1},{1,2},{2,3},{3,4},{4,5},{5,6},{6,7},{7,8},{8,9},{9,10},{10,1... | collective-permute-start | bytes 248 | tf_op jit(solution)/shard_map/while/body/eval_jaxpr/ppermute | solution.py:14
  683.4 76.8 %collective-permute-start = (f32[20,64,64]{2,1,0:T(8,128)}, f32[20,64,64]{2,1,0:T(8,128)}, u32[]{:S(2)}, u32[]{:S(2)}) collective-permute-start(f32[20,64,64]{2,1,0:T(8,128)} %copy.45), channel_id=1, source_target_pairs={{0,1},{1,2},{2,3},{3,4},{4,5},{5,6},{6,7},{7,8},{8,9},{9,10},{10,1... | collective-permute-start | bytes 983048 | tf_op jit(solution)/shard_map/while/body/eval_jaxpr/ppermute | solution.py:14
  683.5 76.7 %collective-permute-start.1 = (s32[20]{0:T(128)S(1)}, s32[20]{0:T(128)S(1)}, u32[]{:S(2)}, u32[]{:S(2)}) collective-permute-start(s32[20]{0:T(128)S(1)} %copy.46), channel_id=1, source_target_pairs={{0,1},{1,2},{2,3},{3,4},{4,5},{5,6},{6,7},{7,8},{8,9},{9,10},{10,1... | collective-permute-start | bytes 248 | tf_op jit(solution)/shard_map/while/body/eval_jaxpr/ppermute | solution.py:14
  762.3 76.2 %collective-permute-start = (f32[20,64,64]{2,1,0:T(8,128)}, f32[20,64,64]{2,1,0:T(8,128)}, u32[]{:S(2)}, u32[]{:S(2)}) collective-permute-start(f32[20,64,64]{2,1,0:T(8,128)} %copy.45), channel_id=1, source_target_pairs={{0,1},{1,2},{2,3},{3,4},{4,5},{5,6},{6,7},{7,8},{8,9},{9,10},{10,1... | collective-permute-start | bytes 983048 | tf_op jit(solution)/shard_map/while/body/eval_jaxpr/ppermute | solution.py:14
  762.4 76.1 %collective-permute-start.1 = (s32[20]{0:T(128)S(1)}, s32[20]{0:T(128)S(1)}, u32[]{:S(2)}, u32[]{:S(2)}) collective-permute-start(s32[20]{0:T(128)S(1)} %copy.46), channel_id=1, source_target_pairs={{0,1},{1,2},{2,3},{3,4},{4,5},{5,6},{6,7},{7,8},{8,9},{9,10},{10,1... | collective-permute-start | bytes 248 | tf_op jit(solution)/shard_map/while/body/eval_jaxpr/ppermute | solution.py:14
  840.5 77.1 %collective-permute-start = (f32[20,64,64]{2,1,0:T(8,128)}, f32[20,64,64]{2,1,0:T(8,128)}, u32[]{:S(2)}, u32[]{:S(2)}) collective-permute-start(f32[20,64,64]{2,1,0:T(8,128)} %copy.45), channel_id=1, source_target_pairs={{0,1},{1,2},{2,3},{3,4},{4,5},{5,6},{6,7},{7,8},{8,9},{9,10},{10,1... | collective-permute-start | bytes 983048 | tf_op jit(solution)/shard_map/while/body/eval_jaxpr/ppermute | solution.py:14
  840.6 77.0 %collective-permute-start.1 = (s32[20]{0:T(128)S(1)}, s32[20]{0:T(128)S(1)}, u32[]{:S(2)}, u32[]{:S(2)}) collective-permute-start(s32[20]{0:T(128)S(1)} %copy.46), channel_id=1, source_target_pairs={{0,1},{1,2},{2,3},{3,4},{4,5},{5,6},{6,7},{7,8},{8,9},{9,10},{10,1... | collective-permute-start | bytes 248 | tf_op jit(solution)/shard_map/while/body/eval_jaxpr/ppermute | solution.py:14
  841.2 76.4 %collective-permute-start.2 = (s32[20]{0:T(128)S(1)}, s32[20]{0:T(128)S(1)}, u32[]{:S(2)}, u32[]{:S(2)}) collective-permute-start(s32[20]{0:T(128)S(1)} %copy.47), channel_id=1, source_target_pairs={{0,1},{1,2},{2,3},{3,4},{4,5},{5,6},{6,7},{7,8},{8,9},{9,10},{10,1... | collective-permute-start | bytes 248 | tf_op jit(solution)/shard_map/while/body/eval_jaxpr/ppermute | solution.py:14
  841.3 76.3 %collective-permute-start.3 = (s32[20]{0:T(128)S(1)}, s32[20]{0:T(128)S(1)}, u32[]{:S(2)}, u32[]{:S(2)}) collective-permute-start(s32[20]{0:T(128)S(1)} %copy.48), channel_id=1, source_target_pairs={{0,1},{1,2},{2,3},{3,4},{4,5},{5,6},{6,7},{7,8},{8,9},{9,10},{10,1... | collective-permute-start | bytes 248 | tf_op jit(solution)/shard_map/while/body/eval_jaxpr/ppermute | solution.py:14
  919.6 77.0 %collective-permute-start = (f32[20,64,64]{2,1,0:T(8,128)}, f32[20,64,64]{2,1,0:T(8,128)}, u32[]{:S(2)}, u32[]{:S(2)}) collective-permute-start(f32[20,64,64]{2,1,0:T(8,128)} %copy.45), channel_id=1, source_target_pairs={{0,1},{1,2},{2,3},{3,4},{4,5},{5,6},{6,7},{7,8},{8,9},{9,10},{10,1... | collective-permute-start | bytes 983048 | tf_op jit(solution)/shard_map/while/body/eval_jaxpr/ppermute | solution.py:14
  919.7 76.9 %collective-permute-start.1 = (s32[20]{0:T(128)S(1)}, s32[20]{0:T(128)S(1)}, u32[]{:S(2)}, u32[]{:S(2)}) collective-permute-start(s32[20]{0:T(128)S(1)} %copy.46), channel_id=1, source_target_pairs={{0,1},{1,2},{2,3},{3,4},{4,5},{5,6},{6,7},{7,8},{8,9},{9,10},{10,1... | collective-permute-start | bytes 248 | tf_op jit(solution)/shard_map/while/body/eval_jaxpr/ppermute | solution.py:14
  920.3 76.3 %collective-permute-start.2 = (s32[20]{0:T(128)S(1)}, s32[20]{0:T(128)S(1)}, u32[]{:S(2)}, u32[]{:S(2)}) collective-permute-start(s32[20]{0:T(128)S(1)} %copy.47), channel_id=1, source_target_pairs={{0,1},{1,2},{2,3},{3,4},{4,5},{5,6},{6,7},{7,8},{8,9},{9,10},{10,1... | collective-permute-start | bytes 248 | tf_op jit(solution)/shard_map/while/body/eval_jaxpr/ppermute | solution.py:14
  920.4 76.2 %collective-permute-start.3 = (s32[20]{0:T(128)S(1)}, s32[20]{0:T(128)S(1)}, u32[]{:S(2)}, u32[]{:S(2)}) collective-permute-start(s32[20]{0:T(128)S(1)} %copy.48), channel_id=1, source_target_pairs={{0,1},{1,2},{2,3},{3,4},{4,5},{5,6},{6,7},{7,8},{8,9},{9,10},{10,1... | collective-permute-start | bytes 248 | tf_op jit(solution)/shard_map/while/body/eval_jaxpr/ppermute | solution.py:14
  998.7 76.9 %collective-permute-start = (f32[20,64,64]{2,1,0:T(8,128)}, f32[20,64,64]{2,1,0:T(8,128)}, u32[]{:S(2)}, u32[]{:S(2)}) collective-permute-start(f32[20,64,64]{2,1,0:T(8,128)} %copy.45), channel_id=1, source_target_pairs={{0,1},{1,2},{2,3},{3,4},{4,5},{5,6},{6,7},{7,8},{8,9},{9,10},{10,1... | collective-permute-start | bytes 983048 | tf_op jit(solution)/shard_map/while/body/eval_jaxpr/ppermute | solution.py:14
  998.8 76.7 %collective-permute-start.1 = (s32[20]{0:T(128)S(1)}, s32[20]{0:T(128)S(1)}, u32[]{:S(2)}, u32[]{:S(2)}) collective-permute-start(s32[20]{0:T(128)S(1)} %copy.46), channel_id=1, source_target_pairs={{0,1},{1,2},{2,3},{3,4},{4,5},{5,6},{6,7},{7,8},{8,9},{9,10},{10,1... | collective-permute-start | bytes 248 | tf_op jit(solution)/shard_map/while/body/eval_jaxpr/ppermute | solution.py:14
  1077.6 76.2 %collective-permute-start = (f32[20,64,64]{2,1,0:T(8,128)}, f32[20,64,64]{2,1,0:T(8,128)}, u32[]{:S(2)}, u32[]{:S(2)}) collective-permute-start(f32[20,64,64]{2,1,0:T(8,128)} %copy.45), channel_id=1, source_target_pairs={{0,1},{1,2},{2,3},{3,4},{4,5},{5,6},{6,7},{7,8},{8,9},{9,10},{10,1... | collective-permute-start | bytes 983048 | tf_op jit(solution)/shard_map/while/body/eval_jaxpr/ppermute | solution.py:14
  1155.9 77.1 %collective-permute-start = (f32[20,64,64]{2,1,0:T(8,128)}, f32[20,64,64]{2,1,0:T(8,128)}, u32[]{:S(2)}, u32[]{:S(2)}) collective-permute-start(f32[20,64,64]{2,1,0:T(8,128)} %copy.45), channel_id=1, source_target_pairs={{0,1},{1,2},{2,3},{3,4},{4,5},{5,6},{6,7},{7,8},{8,9},{9,10},{10,1... | collective-permute-start | bytes 983048 | tf_op jit(solution)/shard_map/while/body/eval_jaxpr/ppermute | solution.py:14
  1155.9 77.0 %collective-permute-start.1 = (s32[20]{0:T(128)S(1)}, s32[20]{0:T(128)S(1)}, u32[]{:S(2)}, u32[]{:S(2)}) collective-permute-start(s32[20]{0:T(128)S(1)} %copy.46), channel_id=1, source_target_pairs={{0,1},{1,2},{2,3},{3,4},{4,5},{5,6},{6,7},{7,8},{8,9},{9,10},{10,1... | collective-permute-start | bytes 248 | tf_op jit(solution)/shard_map/while/body/eval_jaxpr/ppermute | solution.py:14
  1156.5 76.4 %collective-permute-start.2 = (s32[20]{0:T(128)S(1)}, s32[20]{0:T(128)S(1)}, u32[]{:S(2)}, u32[]{:S(2)}) collective-permute-start(s32[20]{0:T(128)S(1)} %copy.47), channel_id=1, source_target_pairs={{0,1},{1,2},{2,3},{3,4},{4,5},{5,6},{6,7},{7,8},{8,9},{9,10},{10,1... | collective-permute-start | bytes 248 | tf_op jit(solution)/shard_map/while/body/eval_jaxpr/ppermute | solution.py:14
  1156.7 76.3 %collective-permute-start.3 = (s32[20]{0:T(128)S(1)}, s32[20]{0:T(128)S(1)}, u32[]{:S(2)}, u32[]{:S(2)}) collective-permute-start(s32[20]{0:T(128)S(1)} %copy.48), channel_id=1, source_target_pairs={{0,1},{1,2},{2,3},{3,4},{4,5},{5,6},{6,7},{7,8},{8,9},{9,10},{10,1... | collective-permute-start | bytes 248 | tf_op jit(solution)/shard_map/while/body/eval_jaxpr/ppermute | solution.py:14
  1235.0 77.0 %collective-permute-start = (f32[20,64,64]{2,1,0:T(8,128)}, f32[20,64,64]{2,1,0:T(8,128)}, u32[]{:S(2)}, u32[]{:S(2)}) collective-permute-start(f32[20,64,64]{2,1,0:T(8,128)} %copy.45), channel_id=1, source_target_pairs={{0,1},{1,2},{2,3},{3,4},{4,5},{5,6},{6,7},{7,8},{8,9},{9,10},{10,1... | collective-permute-start | bytes 983048 | tf_op jit(solution)/shard_map/while/body/eval_jaxpr/ppermute | solution.py:14
  1235.1 76.9 %collective-permute-start.1 = (s32[20]{0:T(128)S(1)}, s32[20]{0:T(128)S(1)}, u32[]{:S(2)}, u32[]{:S(2)}) collective-permute-start(s32[20]{0:T(128)S(1)} %copy.46), channel_id=1, source_target_pairs={{0,1},{1,2},{2,3},{3,4},{4,5},{5,6},{6,7},{7,8},{8,9},{9,10},{10,1... | collective-permute-start | bytes 248 | tf_op jit(solution)/shard_map/while/body/eval_jaxpr/ppermute | solution.py:14
  1235.6 76.4 %collective-permute-start.2 = (s32[20]{0:T(128)S(1)}, s32[20]{0:T(128)S(1)}, u32[]{:S(2)}, u32[]{:S(2)}) collective-permute-start(s32[20]{0:T(128)S(1)} %copy.47), channel_id=1, source_target_pairs={{0,1},{1,2},{2,3},{3,4},{4,5},{5,6},{6,7},{7,8},{8,9},{9,10},{10,1... | collective-permute-start | bytes 248 | tf_op jit(solution)/shard_map/while/body/eval_jaxpr/ppermute | solution.py:14
  1235.7 76.3 %collective-permute-start.3 = (s32[20]{0:T(128)S(1)}, s32[20]{0:T(128)S(1)}, u32[]{:S(2)}, u32[]{:S(2)}) collective-permute-start(s32[20]{0:T(128)S(1)} %copy.48), channel_id=1, source_target_pairs={{0,1},{1,2},{2,3},{3,4},{4,5},{5,6},{6,7},{7,8},{8,9},{9,10},{10,1... | collective-permute-start | bytes 248 | tf_op jit(solution)/shard_map/while/body/eval_jaxpr/ppermute | solution.py:14
  1314.1 76.9 %collective-permute-start = (f32[20,64,64]{2,1,0:T(8,128)}, f32[20,64,64]{2,1,0:T(8,128)}, u32[]{:S(2)}, u32[]{:S(2)}) collective-permute-start(f32[20,64,64]{2,1,0:T(8,128)} %copy.45), channel_id=1, source_target_pairs={{0,1},{1,2},{2,3},{3,4},{4,5},{5,6},{6,7},{7,8},{8,9},{9,10},{10,1... | collective-permute-start | bytes 983048 | tf_op jit(solution)/shard_map/while/body/eval_jaxpr/ppermute | solution.py:14
  1314.2 76.8 %collective-permute-start.1 = (s32[20]{0:T(128)S(1)}, s32[20]{0:T(128)S(1)}, u32[]{:S(2)}, u32[]{:S(2)}) collective-permute-start(s32[20]{0:T(128)S(1)} %copy.46), channel_id=1, source_target_pairs={{0,1},{1,2},{2,3},{3,4},{4,5},{5,6},{6,7},{7,8},{8,9},{9,10},{10,1... | collective-permute-start | bytes 248 | tf_op jit(solution)/shard_map/while/body/eval_jaxpr/ppermute | solution.py:14
  (19 other events, 1043.8 us)
Sparse Core Ops, SparseCore 0:
  9.7 185.3 all-gather.1
where the time goes:
time: 1490 us; the launch traced here: 1470 us
  local copies, waits for them, and re-layouts  943 us (63%)
  other arithmetic  183 us (12%)
  waiting for transfers between devices  168 us (11%)
  matrix products  104 us (7%)
  starting transfers between devices  43.6 us (3%)
    scatter-add x16, local copies, waits for them, and re-layouts, product_panel(): dense_b.at[right_row - k_first, :, right_col - col_first, :].add(right_blk)  322 us
    reshape x16, local copies, waits for them, and re-layouts, product_panel(): dense_b = dense_b.reshape(group_span * block_size, CW * block_size)  227 us
    all_gather x1, waiting for transfers between devices, on_device(): lax.all_gather(b_blocks, 'row', axis=0, tiled=True)  168 us
    another operation x32, local copies, waits for them, and re-layouts  165 us
    scatter-add x16, local copies, waits for them, and re-layouts, dense_left(): panel = panel.at[left_row - row_first, :, left_col - k_first, :].add(scaled)  105 us
    dot_general x16, matrix products, product_panel(): jnp.dot(left_dense, dense_b, precision=lax.Precision.HIGHEST, preferred_e...  104 us
    scatter-add x16, other arithmetic, dense_left(): panel = panel.at[left_row - row_first, :, left_col - k_first, :].add(scaled)  81.8 us
    scatter-add x16, other arithmetic, product_panel(): dense_b.at[right_row - k_first, :, right_col - col_first, :].add(right_blk)  81.3 us
  transfers between devices with their start and end apart: 61, of which 1 were waited for; matrix products, arithmetic and copies ran while one was open for 76% of the time, Pallas kernels for 0%

commit v1 on v0

v1 whole, which is shorter than its diff:
```python
import functools

import jax
import jax.numpy as jnp
from jax import lax
from jax.experimental import pallas as pl
from jax.experimental.pallas import tpu as pltpu
from jax.sharding import PartitionSpec as P

MESH = pl.DeviceIdType.MESH
BS = 64
KG = 64
RW = 2
CW = 8
SA = 20
SB = 64
PAIRS = SA // 2
ROWS = PAIRS * BS
PIECE = ROWS // 16
SEG = 2 * PIECE
PLANE = ROWS // 2
CHUNKS = 8
F32 = jnp.float32
BF16 = jnp.bfloat16


def split(value):
    high = value.astype(BF16)
    low = (value - high.astype(F32)).astype(BF16)
    return high, low


def kernel(
    a_rows, a_cols, a_keep, b_rows, b_cols, a_hbm, b_hbm, out,
    a_raw, packed, a_all, b_raw, left_hi, left_lo, right_hi, right_lo, dense_hi, dense_lo,
    meta_out, meta_in, meta_rows, meta_s, table_v, table_s,
    c_part, c_z, c_x_out, c_x_in,
    load_sem, smem_sem, scat_send, scat_recv, meta_send, meta_recv,
    x_send, x_recv, y_send, y_recv, f_send, f_recv, core_send, core_recv,
    z_send, z_recv, h_send, h_recv,
):
    r = lax.axis_index("row")
    c = lax.axis_index("col")
    x_hi, z = r // 4, r % 4
    y, x_lo, core = c // 4, (c // 2) % 2, c % 2
    kappa, half = c % 8, c // 8
    local_target = kappa == r
    sibling = (r, y * 4 + x_lo * 2 + (1 - core))
    x_near = (r, y * 4 + (1 - x_lo) * 2 + core)
    y_up = (r, ((y + 1) % 4) * 4 + x_lo * 2 + core)
    y_down = (r, ((y + 3) % 4) * 4 + x_lo * 2 + core)
    x_far = ((1 - x_hi) * 4 + z, c)
    z_peer = [(x_hi * 4 + (z + d) % 4, c) for d in range(4)]

    load_b = pltpu.make_async_copy(b_hbm, b_raw, load_sem.at[1])
    load_a = pltpu.make_async_copy(a_hbm, a_raw, load_sem.at[0])
    load_a.start()
    load_b.start()

    barrier = pltpu.get_barrier_semaphore()
    for peer in (sibling, x_near, y_up, y_down, x_far, z_peer[1], z_peer[2], z_peer[3]):
        pl.semaphore_signal(barrier, inc=1, device_id=peer, device_id_type=MESH)

    def greet(i, carry):
        source = (i // 2, r + 8 * (i % 2))

        @pl.when(jnp.logical_or(source[0] != r, source[1] != c))
        def _():
            pl.semaphore_signal(barrier, inc=1, device_id=source, device_id_type=MESH)

        return carry

    lax.fori_loop(0, 16, greet, 0)

    lane = lax.broadcasted_iota(jnp.int32, (8, 128), 1)
    sub = lax.broadcasted_iota(jnp.int32, (8, 128), 0)
    meta = jnp.zeros((8, 128), jnp.int32)
    for a in range(SA):
        keep = a_keep[a]
        low_row = lax.rem(a_rows[a], RW)
        meta = jnp.where(lane == a, lax.rem(a_cols[a], KG) + half * KG, meta)
        meta = jnp.where(lane == 32 + a, keep * (1 - low_row), meta)
        meta = jnp.where(lane == 64 + a, keep * low_row, meta)
    meta_out[...] = meta

    load_a.wait()
    for p in range(PAIRS):
        packed[pl.ds(p * BS, BS), :] = jnp.concatenate([a_raw[2 * p], a_raw[2 * p + 1]], axis=1)

    @pl.when(local_target)
    def _():
        pl.semaphore_wait(barrier, 23)

    @pl.when(jnp.logical_not(local_target))
    def _():
        pl.semaphore_wait(barrier, 24)

    run = r * 2 + half

    def scatter(p, carry):
        target = (kappa, ((p // 2) % 4) * 4 + (p % 2) * 2 + p // 8)
        rows = pl.ds(pl.multiple_of(p * PIECE, 8), PIECE)
        here = jnp.logical_and(target[0] == r, target[1] == c)

        @pl.when(here)
        def _():
            pltpu.make_async_copy(packed.at[rows], a_all.at[run, rows], scat_recv.at[r]).start()
            pltpu.make_async_copy(meta_out, meta_in.at[run], meta_recv).start()

        @pl.when(jnp.logical_not(here))
        def _():
            pltpu.make_async_remote_copy(
                packed.at[rows], a_all.at[run, rows], scat_send, scat_recv.at[r],
                device_id=target, device_id_type=MESH,
            ).start()
            pltpu.make_async_remote_copy(
                meta_out, meta_in.at[run], meta_send, meta_recv,
                device_id=target, device_id_type=MESH,
            ).start()

        return carry

    lax.fori_loop(0, 16, scatter, 0)

    flat = sub * 128 + lane
    table = jnp.full((8, 128), SB, jnp.int32)
    for s in range(SB):
        inner = lax.rem(b_rows[s], KG) + (0 if s < SB // 2 else KG)
        place = inner * CW + lax.rem(b_cols[s], CW)
        table = jnp.where(flat == place, s, table)
    table_v[...] = table
    table_copy = pltpu.make_async_copy(table_v, table_s, smem_sem.at[0])
    table_copy.start()

    def chunk_of(t):
        return (x_hi + 1 - t // 4) % 2 * 4 + (z + t % 4 + 1) % 4

    own_rows = pl.ds(pl.multiple_of(core * PLANE + y * SEG + x_lo * PIECE, 8), PIECE)

    def seg_rows(where):
        return pl.ds(pl.multiple_of(core * PLANE + where * SEG, 8), SEG)

    def remote(src, dst, send, recv, peer):
        return pltpu.make_async_remote_copy(src, dst, send, recv, device_id=peer, device_id_type=MESH)

    def same(ref, send, recv, peer):
        return remote(ref, ref, send, recv, peer)

    def stage_x(t, carry):
        ch = chunk_of(t)
        mine = a_all.at[pl.ds(2 * ch, 2), own_rows]
        same(mine, x_send, scat_recv.at[ch], x_near).wait_recv()
        same(mine, x_send, x_recv.at[t], x_near).start()
        return carry

    def stage_y(t):
        ch = chunk_of(t)
        mine = a_all.at[pl.ds(2 * ch, 2), own_rows]
        same(mine, x_send, x_recv.at[t], x_near).wait_recv()
        seg = a_all.at[pl.ds(2 * ch, 2), seg_rows(y)]
        same(seg, y_send.at[0], y_recv.at[0, t], y_up).start()
        same(seg, y_send.at[1], y_recv.at[1, t], y_down).start()

    def stage_f(t):
        ch = chunk_of(t)
        below = a_all.at[pl.ds(2 * ch, 2), seg_rows((y + 3) % 4)]
        same(below, y_send.at[0], y_recv.at[0, t], y_up).wait_recv()
        half_below = a_all.at[2 * ch, seg_rows((y + 3) % 4)]
        same(half_below, f_send.at[0], f_recv.at[0, t], y_up).start()
        above = a_all.at[pl.ds(2 * ch, 2), seg_rows((y + 1) % 4)]
        same(above, y_send.at[1], y_recv.at[1, t], y_down).wait_recv()
        half_above = a_all.at[2 * ch + 1, seg_rows((y + 1) % 4)]
        same(half_above, f_send.at[1], f_recv.at[1, t], y_down).start()

    plane_rows = pl.ds(pl.multiple_of(core * PLANE, 8), PLANE)
    far_rows = seg_rows((y + 2) % 4)

    def stage_core(t):
        ch = chunk_of(t)
        same(a_all.at[2 * ch, far_rows], f_send.at[0], f_recv.at[0, t], y_up).wait_recv()
        same(a_all.at[2 * ch + 1, far_rows], f_send.at[1], f_recv.at[1, t], y_down).wait_recv()
        same(a_all.at[pl.ds(2 * ch, 2), plane_rows], core_send, core_recv.at[t], sibling).start()

    pair_lane = lax.broadcasted_iota(jnp.int32, (1, 128), 1) < BS

    def pair_mask(run_at, base, p):
        first = meta_s[run_at, base + 2 * p].astype(F32)
        second = meta_s[run_at, base + 2 * p + 1].astype(F32)
        return jnp.where(pair_lane, first, second)

    def stage_product(t):
        ch = chunk_of(t)
        same(a_all.at[pl.ds(2 * ch, 2), plane_rows], core_send, core_recv.at[t], sibling).wait_recv()
        total = jnp.zeros((RW * BS, CW * BS), F32)
        for h in range(2):
            at = 2 * ch + h
            for g in range(PAIRS // 2):
                block = jnp.concatenate(
                    [a_all[at, pl.ds((2 * g + i) * BS, BS), :] for i in range(2)], axis=1
                )
                high, low = split(block)
                masks = [
                    jnp.concatenate([pair_mask(at, base, 2 * g + i) for i in range(2)], axis=1).astype(BF16)
                    for base in (32, 64)
                ]
                left_high = jnp.concatenate([high * m for m in masks], axis=0)
                left_low = jnp.concatenate([low * m for m in masks], axis=0)
                inner = [meta_s[at, 4 * g + i] for i in range(4)]
                right_high = jnp.concatenate([dense_hi[k] for k in inner], axis=0)
                right_low = jnp.concatenate([dense_lo[k] for k in inner], axis=0)
                total += jnp.dot(left_high, right_high, preferred_element_type=F32)
                total += jnp.dot(left_low, right_high, preferred_element_type=F32)
                total += jnp.dot(left_high, right_low, preferred_element_type=F32)
        c_part[t] = total
        d = (t + 1) % 4

        @pl.when(d != 0)
        def _():
            remote(
                c_part.at[t], c_z.at[t], z_send.at[t], z_recv.at[t], (x_hi * 4 + (z + d) % 4, c)
            ).start()

    def build(k, carry):
        for j in range(CW // 2):
            first = table_s[k // 16, (k % 16) * CW + 2 * j]
            second = table_s[k // 16, (k % 16) * CW + 2 * j + 1]
            dense_hi[k, :, pl.ds(j * 128, 128)] = left_hi[first] + right_hi[second]
            dense_lo[k, :, pl.ds(j * 128, 128)] = left_lo[first] + right_lo[second]
        return carry

    load_b.wait()
    blank = jnp.zeros((BS, BS), F32)

    def widen(s, carry):
        value = b_raw[s]
        left_hi[s], left_lo[s] = split(jnp.concatenate([value, blank], axis=1))
        right_hi[s], right_lo[s] = split(jnp.concatenate([blank, value], axis=1))
        return carry

    lax.fori_loop(0, SB, widen, 0)
    for ref in (left_hi, left_lo, right_hi, right_lo):
        ref[SB] = jnp.zeros((BS, 2 * BS), BF16)

    lax.fori_loop(0, CHUNKS, stage_x, 0)
    table_copy.wait()
    stage_y(0)
    stage_y(1)
    lax.fori_loop(0, KG, build, 0)
    stage_f(0)
    lax.fori_loop(KG, 2 * KG, build, 0)

    pltpu.make_async_copy(meta_in, meta_in, meta_recv).wait()
    for i in range(16):
        meta_rows[pl.ds(i, 1), :] = meta_in[i, pl.ds(0, 1), :]
    meta_copy = pltpu.make_async_copy(meta_rows, meta_s, smem_sem.at[1])
    meta_copy.start()
    meta_copy.wait()

    def step(t, carry):
        @pl.when(t < CHUNKS - 2)
        def _():
            stage_y(t + 2)

        @pl.when(t < CHUNKS - 1)
        def _():
            stage_f(t + 1)

        @pl.when(t < CHUNKS)
        def _():
            stage_core(t)

        @pl.when(t > 0)
        def _():
            stage_product(t - 1)

        @pl.when(t == 6)
        def _():
            for i in range(3):
                remote(c_part.at[i], c_z.at[i], z_send.at[i], z_recv.at[i], x_far).wait_recv()
            c_x_out[...] = (c_part[3] + c_z[0]) + (c_z[1] + c_z[2])
            remote(c_x_out, c_x_in, h_send, h_recv, x_far).start()

        return carry

    lax.fori_loop(0, CHUNKS + 1, step, 0)

    for i in range(4, 7):
        remote(c_part.at[i], c_z.at[i], z_send.at[i], z_recv.at[i], x_far).wait_recv()
    mine = (c_part[7] + c_z[4]) + (c_z[5] + c_z[6])
    remote(c_x_out, c_x_in, h_send, h_recv, x_far).wait_recv()
    out[...] = mine + c_x_in[...]

    def sent(ref, sem):
        remote(ref, ref, sem, h_recv, x_far).wait_send()

    @pl.when(local_target)
    def _():
        sent(packed.at[pl.ds(0, ROWS - PIECE)], scat_send)
        sent(meta_in.at[pl.ds(0, 15)], meta_send)

    @pl.when(jnp.logical_not(local_target))
    def _():
        sent(packed, scat_send)
        sent(meta_in, meta_send)

    sent(a_all.at[:, own_rows], x_send)
    for i in range(2):
        sent(a_all.at[:, seg_rows(y)], y_send.at[i])
        sent(a_all.at[pl.ds(0, CHUNKS), seg_rows(y)], f_send.at[i])
    sent(a_all.at[:, plane_rows], core_send)
    for i in (0, 1, 2, 4, 5, 6):
        sent(c_part.at[i], z_send.at[i])
    sent(c_x_out, h_send)


def on_device(a_blocks, a_rows, a_cols, a_keep, b_blocks, b_rows, b_cols):
    dma = pltpu.SemaphoreType.DMA
    return pl.pallas_call(
        kernel,
        out_shape=jax.ShapeDtypeStruct((RW * BS, CW * BS), F32),
        in_specs=[pl.BlockSpec(memory_space=pltpu.SMEM)] * 5 + [pl.BlockSpec(memory_space=pl.ANY)] * 2,
        out_specs=pl.BlockSpec(memory_space=pltpu.VMEM),
        scratch_shapes=[
            pltpu.VMEM((SA, BS, BS), F32),
            pltpu.VMEM((ROWS, 128), F32),
            pltpu.VMEM((16, ROWS, 128), F32),
            pltpu.VMEM((SB, BS, BS), F32),
            pltpu.VMEM((SB + 1, BS, 128), BF16),
            pltpu.VMEM((SB + 1, BS, 128), BF16),
            pltpu.VMEM((SB + 1, BS, 128), BF16),
            pltpu.VMEM((SB + 1, BS, 128), BF16),
            pltpu.VMEM((2 * KG, BS, CW * BS), BF16),
            pltpu.VMEM((2 * KG, BS, CW * BS), BF16),
            pltpu.VMEM((8, 128), jnp.int32),
            pltpu.VMEM((16, 8, 128), jnp.int32),
            pltpu.VMEM((16, 128), jnp.int32),
            pltpu.SMEM((16, 128), jnp.int32),
            pltpu.VMEM((8, 128), jnp.int32),
            pltpu.SMEM((8, 128), jnp.int32),
            pltpu.VMEM((CHUNKS, RW * BS, CW * BS), F32),
            pltpu.VMEM((CHUNKS, RW * BS, CW * BS), F32),
            pltpu.VMEM((RW * BS, CW * BS), F32),
            pltpu.VMEM((RW * BS, CW * BS), F32),
            dma((2,)), dma((2,)), dma, dma((CHUNKS,)), dma, dma,
            dma, dma((CHUNKS,)), dma((2,)), dma((2, CHUNKS)), dma((2,)), dma((2, CHUNKS)),
            dma, dma((CHUNKS,)),
            dma((CHUNKS,)), dma((CHUNKS,)), dma, dma,
        ],
        compiler_params=pltpu.CompilerParams(
            collective_id=0, has_side_effects=True, vmem_limit_bytes=56 * 1024 * 1024
        ),
        cost_estimate=pl.CostEstimate(flops=2 * 3 * 1024 * 2560 * 512, bytes_accessed=8 << 20, transcendentals=0),
    )(a_rows, a_cols, a_keep, b_rows, b_cols, a_blocks, b_blocks)


def solution(mesh):
    in_specs = (
        P(("row", "col"), None, None),
        P(("row", "col")),
        P(("row", "col")),
        P(("row", "col")),
        P(("row", "col"), None, None),
        P(("row", "col")),
        P(("row", "col")),
    )
    return jax.shard_map(
        on_device, mesh=mesh, in_specs=in_specs, out_specs=P("row", "col"), check_vma=False
    )
```

time: 1490 us -> 68.7 us (0.05); the launches traced: 1470 us -> 67.9 us
  local copies, waits for them, and re-layouts: 943 us -> 1.67 us
  other arithmetic: 183 us -> 0 us
  waiting for transfers between devices: 168 us -> 0 us
  matrix products: 104 us -> 0 us
  Pallas kernels: 0 us -> 66.2 us
  starting transfers between devices: 43.6 us -> 0 us
    scatter-add x32 -> x0, local copies, waits for them, and re-layouts: 427 us -> none  [the longest x16 322 us: product_panel(): dense_b.at[right_row - k_first, :, right_col - col_first, :].add(right_blk)]
    reshape x35 -> x0, local copies, waits for them, and re-layouts: 284 us -> none  [the longest x16 227 us: product_panel(): dense_b = dense_b.reshape(group_span * block_size, CW * block_size)]
    all_gather x1 -> x0, waiting for transfers between devices: 168 us -> none  [on_device(): lax.all_gather(b_blocks, 'row', axis=0, tiled=True)]
    another operation x32 -> x0, local copies, waits for them, and re-layouts: 165 us -> none
    scatter-add x32 -> x0, other arithmetic: 163 us -> none  [the longest x16 81.8 us: dense_left(): panel = panel.at[left_row - row_first, :, left_col - k_first, :].add(scaled)]
    dot_general x16 -> x0, matrix products: 104 us -> none  [product_panel(): jnp.dot(left_dense, dense_b, precision=lax.Precision.HIGHEST, preferred_e...]
    pallas_call x0 -> x1, Pallas kernels: none -> 66.2 us  [on_device(): pl.pallas_call(kernel, out_shape=jax.ShapeDtypeStruct((RW * BS, CW * BS),...]
    ppermute x60 -> x0, starting transfers between devices: 43.6 us -> none  [from_behind(): return lax.ppermute(value, axis, pairs)]
  transfers between devices with their start and end apart: 61 -> 0, of which waited for: 1 -> 0; matrix products, arithmetic and copies ran while one was open for 76% -> 0% of each run, Pallas kernels for 0% -> 0%
where the time goes in v1:
time: 68.7 us; the launch traced here: 67.9 us
  Pallas kernels  66.2 us (96%)
  local copies, waits for them, and re-layouts  1.67 us (2%)
    pallas_call x1, Pallas kernels, on_device(): pl.pallas_call(kernel, out_shape=jax.ShapeDtypeStruct((RW * BS, CW * BS),...  66.2 us
    unnamed x1, local copies, waits for them, and re-layouts  1.67 us

profile of v1, /device:TPU:0, one launch (start us, length us, event | category | flops | bytes accessed | tf_op | source)
XLA Modules:
  0.0 67.9 jit_solution(12386353225200462879)
XLA Ops:
  0.0 66.2 %shard_map.73 = f32[128,512]{1,0:T(8,128)} custom-call(s32[20]{0:T(128)} %a_rows.1, s32[20]{0:T(128)} %a_cols.1, s32[20]{0:T(128)} %a_keep.1, s32[64]{0:T(128)} %b_rows.1, s32[64]{0:T(128)} %b_cols.1, f32[20,64,64]{2,1,0:T(8,128)} %a_hbm.1, f32[64,64,64]{2,1,0:T(8,128)} %b_hbm.1), custom_call_target="tpu_custom_call" | custom-call | flops 8053063680 | bytes 8388608 | tf_op jit(solution)/shard_map/pallas_call | solution.py:318
  66.2 1.7 %copy.9 = f32[128,512]{1,0:T(8,128)} copy(f32[128,512]{1,0:T(8,128)} %shard_map.73) | data formatting | bytes 524288

commit v2 on v1

v2 whole, which is shorter than its diff:
```python
import functools

import jax
import jax.numpy as jnp
from jax import lax
from jax.experimental import pallas as pl
from jax.experimental.pallas import tpu as pltpu
from jax.sharding import PartitionSpec as P

MESH = pl.DeviceIdType.MESH
BS = 64
KG = 64
RW = 2
CW = 8
SA = 20
SB = 64
PAIRS = SA // 2
ROWS = PAIRS * BS
PIECE = ROWS // 8
HALF = PIECE // 2
CHUNKS = 8
LATE = 3
EARLY = CHUNKS - LATE
UNROLL = 2
F32 = jnp.float32
BF16 = jnp.bfloat16


def split(value):
    high = value.astype(BF16)
    low = (value - high.astype(F32)).astype(BF16)
    return high, low


def kernel(
    a_rows, a_cols, a_keep, b_rows, b_cols, a_hbm, b_hbm, out,
    a_raw, packed, a_all, b_raw, twice_hi, twice_lo, dense_hi, dense_lo,
    meta_out, meta_in, meta_v, meta_s, table_v, table_s,
    c_part, z_half, z_full, c_x_out, c_x_in,
    load_sem, smem_sem, scat_send, scat_recv, meta_send, meta_recv, meta_swap_send, meta_swap_recv,
    x_send, x_recv, own_send, own_recv, near_send, near_recv, pass_send, pass_half_send, pass_recv,
    core_send, core_recv, zh_send, zh_recv, zf_send, zf_recv, h_send, h_recv,
):
    r = lax.axis_index("row")
    c = lax.axis_index("col")
    x_hi, z = r // 4, r % 4
    y, x_lo, core = c // 4, (c // 2) % 2, c % 2
    kappa, half = c % 8, c // 8
    local_target = jnp.logical_and(kappa == r, half == core)
    sibling = (r, y * 4 + x_lo * 2 + (1 - core))
    x_near = (r, y * 4 + (1 - x_lo) * 2 + core)
    y_way = [(r, ((y + 1) % 4) * 4 + x_lo * 2 + core), (r, ((y + 3) % 4) * 4 + x_lo * 2 + core)]
    z_way = [(x_hi * 4 + (z + 1) % 4, c), (x_hi * 4 + (z + 3) % 4, c)]
    x_far = ((1 - x_hi) * 4 + z, c)

    barrier = pltpu.get_barrier_semaphore()

    def greet(i, carry):
        @pl.when(jnp.logical_or(i != r, r + 8 * core != c))
        def _():
            pl.semaphore_signal(barrier, inc=1, device_id=(i, r + 8 * core), device_id_type=MESH)

        return carry

    lax.fori_loop(0, 8, greet, 0)
    for peer in (x_far, *z_way, *y_way, x_near, sibling):
        pl.semaphore_signal(barrier, inc=1, device_id=peer, device_id_type=MESH)

    load_a = pltpu.make_async_copy(a_hbm, a_raw, load_sem.at[0])
    load_b = pltpu.make_async_copy(b_hbm, b_raw, load_sem.at[1])
    load_a.start()
    load_b.start()

    lane = lax.broadcasted_iota(jnp.int32, (8, 128), 1)
    sub = lax.broadcasted_iota(jnp.int32, (8, 128), 0)
    meta = jnp.zeros((8, 128), jnp.int32)
    for a in range(SA):
        keep = a_keep[a]
        low_row = lax.rem(a_rows[a], RW)
        meta = jnp.where(lane == a, lax.rem(a_cols[a], KG) + half * KG, meta)
        meta = jnp.where(lane == 32 + a, keep * (1 - low_row), meta)
        meta = jnp.where(lane == 64 + a, keep * low_row, meta)
    meta_out[...] = meta

    load_a.wait()
    for p in range(PAIRS):
        packed[pl.ds(p * BS, BS), :] = jnp.concatenate([a_raw[2 * p], a_raw[2 * p + 1]], axis=1)

    @pl.when(local_target)
    def _():
        pl.semaphore_wait(barrier, 14)

    @pl.when(jnp.logical_not(local_target))
    def _():
        pl.semaphore_wait(barrier, 15)

    run = r * 2 + half

    def remote(src, dst, send, recv, peer):
        return pltpu.make_async_remote_copy(src, dst, send, recv, device_id=peer, device_id_type=MESH)

    def same(ref, send, recv, peer):
        return remote(ref, ref, send, recv, peer)

    def scatter(p, carry):
        target = (kappa, (p // 2) * 4 + (p % 2) * 2 + half)
        piece = packed.at[pl.ds(pl.multiple_of(p * PIECE, 16), PIECE)]
        place = a_all.at[run, p // 2, p % 2]
        here = jnp.logical_and(target[0] == r, target[1] == c)

        @pl.when(here)
        def _():
            pltpu.make_async_copy(piece, place, scat_recv.at[r]).start()
            pltpu.make_async_copy(meta_out, meta_in.at[r], meta_recv).start()

        @pl.when(jnp.logical_not(here))
        def _():
            remote(piece, place, scat_send, scat_recv.at[r], target).start()
            remote(meta_out, meta_in.at[r], meta_send, meta_recv, target).start()

        return carry

    lax.fori_loop(0, 8, scatter, 0)

    flat = sub * 128 + lane
    table = jnp.full((8, 128), SB, jnp.int32)
    for s in range(SB):
        inner = lax.rem(b_rows[s], KG) + (0 if s < SB // 2 else KG)
        place = inner * CW + lax.rem(b_cols[s], CW)
        table = jnp.where(flat == place, s, table)
    table_v[...] = table
    table_copy = pltpu.make_async_copy(table_v, table_s, smem_sem.at[0])
    table_copy.start()

    def chunk_of(t):
        turn = t % 4
        away = (2 + turn + (turn // 2) * (5 - 2 * turn)) % 4
        return (x_hi + 1 - t // 4) % 2 * 4 + (z + away) % 4

    def plane(t):
        return a_all.at[2 * chunk_of(t) + core]

    def crosses_late(t):
        return t >= EARLY

    def own(t):
        return plane(t).at[y, x_lo]

    def stage_own(t):
        piece = own(t)
        same(piece, own_send.at[0], scat_recv.at[chunk_of(t)], x_near).wait_recv()
        for way in range(2):
            same(piece, own_send.at[way], own_recv.at[way, t], y_way[way]).start()
        if not crosses_late(t):
            same(piece, x_send.at[0], x_recv.at[t], x_near).start()

    def stage_near(t):
        if t < EARLY:
            piece = plane(t).at[y, 1 - x_lo]
            same(piece, x_send.at[0], x_recv.at[t], x_near).wait_recv()
            for way in range(2):
                same(piece, near_send.at[way], near_recv.at[way, t], y_way[way]).start()

    def stage_pass(t):
        below = plane(t).at[(y + 3) % 4]
        above = plane(t).at[(y + 1) % 4]
        if crosses_late(t):
            for way, column in ((0, below), (1, above)):
                piece = column.at[x_lo]
                same(piece, own_send.at[way], own_recv.at[way, t], y_way[way]).wait_recv()
                part = piece.at[pl.ds(way * HALF, HALF)]
                same(part, pass_half_send.at[way], pass_recv.at[way, t], y_way[way]).start()
        else:
            same(below.at[x_lo], own_send.at[0], own_recv.at[0, t], y_way[0]).wait_recv()
            same(below.at[x_lo], pass_send.at[0], pass_recv.at[0, t], y_way[0]).start()
            same(above.at[1 - x_lo], near_send.at[1], near_recv.at[1, t], y_way[1]).wait_recv()
            same(above.at[1 - x_lo], pass_send.at[1], pass_recv.at[1, t], y_way[1]).start()

    def to_sibling(t):
        same(plane(t), core_send, core_recv.at[t], sibling).start()

    def stage_far(t):
        far = plane(t).at[(y + 2) % 4]
        if crosses_late(t):
            for way in range(2):
                part = far.at[x_lo, pl.ds(way * HALF, HALF)]
                same(part, pass_half_send.at[way], pass_recv.at[way, t], y_way[way]).wait_recv()
            same(plane(t).at[:, x_lo], x_send.at[1], x_recv.at[t], x_near).start()
        else:
            above = plane(t).at[(y + 1) % 4]
            below = plane(t).at[(y + 3) % 4]
            same(above.at[x_lo], own_send.at[1], own_recv.at[1, t], y_way[1]).wait_recv()
            same(below.at[1 - x_lo], near_send.at[0], near_recv.at[0, t], y_way[0]).wait_recv()
            same(far.at[x_lo], pass_send.at[0], pass_recv.at[0, t], y_way[0]).wait_recv()
            same(far.at[1 - x_lo], pass_send.at[1], pass_recv.at[1, t], y_way[1]).wait_recv()
            to_sibling(t)

    def stage_late(t):
        same(plane(t).at[:, 1 - x_lo], x_send.at[1], x_recv.at[t], x_near).wait_recv()
        to_sibling(t)

    pair_lane = lax.broadcasted_iota(jnp.int32, (1, 128), 1) < BS

    def pair_mask(h, ch, base, p):
        first = meta_s[h, ch, base + 2 * p].astype(F32)
        second = meta_s[h, ch, base + 2 * p + 1].astype(F32)
        return jnp.where(pair_lane, first, second)

    def pair_rows(at, p):
        parts, start, end = [], p * BS, (p + 1) * BS
        while start < end:
            piece, offset = divmod(start, PIECE)
            count = min(end - start, PIECE - offset)
            parts.append(a_all[at, piece // 2, piece % 2, pl.ds(offset, count), :])
            start += count
        return jnp.concatenate(parts, axis=0)

    def stage_product(t):
        ch = chunk_of(t)
        same(a_all.at[2 * ch + 1 - core], core_send, core_recv.at[t], sibling).wait_recv()
        total = jnp.zeros((RW * BS, CW * BS), F32)
        for h in range(2):
            for g in range(PAIRS // 2):
                block = jnp.concatenate([pair_rows(2 * ch + h, 2 * g + i) for i in range(2)], axis=1)
                high, low = split(block)
                masks = [
                    jnp.concatenate([pair_mask(h, ch, base, 2 * g + i) for i in range(2)], axis=1).astype(BF16)
                    for base in (32, 64)
                ]
                left_high = jnp.concatenate([high * m for m in masks], axis=0)
                left_low = jnp.concatenate([low * m for m in masks], axis=0)
                inner = [meta_s[h, ch, 4 * g + i] for i in range(4)]
                right_high = jnp.concatenate([dense_hi[k] for k in inner], axis=0)
                right_low = jnp.concatenate([dense_lo[k] for k in inner], axis=0)
                total += jnp.dot(left_high, right_high, preferred_element_type=F32)
                total += jnp.dot(left_low, right_high, preferred_element_type=F32)
                total += jnp.dot(left_high, right_low, preferred_element_type=F32)
        c_part[t] = total

    def part_rows(way):
        return pl.ds(way * BS, BS)

    def z_farthest(e, way):
        return remote(
            c_part.at[4 * e, part_rows(way)], z_half.at[e, way],
            zh_send.at[e, way], zh_recv.at[e, way], z_way[way],
        )

    def z_next(e, way):
        return remote(
            c_part.at[4 * e + 2 - way], z_full.at[e, way],
            zf_send.at[e, way], zf_recv.at[e, way], z_way[way],
        )

    def sum_along(t):
        e = t // 4

        @pl.when(t % 4 == 0)
        def _():
            for way in range(2):
                z_farthest(e, way).start()

        @pl.when(t % 4 == 2)
        def _():
            for way in (1, 0):
                z_farthest(e, way).wait_recv()
                c_part[4 * e + 2 - way, part_rows(way), :] += z_half[e, way]
                z_next(e, way).start()

        @pl.when(t == 5)
        def _():
            for way in range(2):
                z_next(0, way).wait_recv()
            c_x_out[...] = c_part[3] + z_full[0, 0] + z_full[0, 1]
            remote(c_x_out, c_x_in, h_send, h_recv, x_far).start()

    first_half = lax.broadcasted_iota(jnp.int32, (BS, 2 * BS), 1) < BS

    def build(step, carry):
        for u in range(UNROLL):
            k = step * UNROLL + u
            slots = [table_s[k // 16, (k % 16) * CW + j] for j in range(CW)]
            for dense, twice in ((dense_hi, twice_hi), (dense_lo, twice_lo)):
                tiles = [
                    jnp.where(first_half, twice[slots[j]], twice[slots[j + 1]]) for j in range(0, CW, 2)
                ]
                dense[k] = jnp.concatenate(tiles, axis=1)
        return carry

    def build_some(start, end):
        lax.fori_loop(start // UNROLL, end // UNROLL, build, 0)

    load_b.wait()

    def widen(step, carry):
        for u in range(4):
            s = step * 4 + u
            value = b_raw[s]
            twice_hi[s], twice_lo[s] = split(jnp.concatenate([value, value], axis=1))
        return carry

    lax.fori_loop(0, SB // 4, widen, 0)
    for ref in (twice_hi, twice_lo):
        ref[SB] = jnp.zeros((BS, 2 * BS), BF16)

    late = range(EARLY, CHUNKS)
    def meta_pass_on():
        pltpu.make_async_copy(meta_in, meta_in, meta_recv).wait()
        for i in range(8):
            meta_v[core, pl.ds(i, 1), :] = meta_in[i, pl.ds(0, 1), :]
        same(meta_v.at[core], meta_swap_send, meta_swap_recv, sibling).start()

    meta_copy = pltpu.make_async_copy(meta_v, meta_s, smem_sem.at[1])

    def meta_take():
        same(meta_v.at[1 - core], meta_swap_send, meta_swap_recv, sibling).wait_recv()
        meta_copy.start()

    table_copy.wait()
    build_some(0, 64)
    stage_own(7)
    stage_own(5)
    stage_own(6)
    stage_own(4)
    stage_own(3)
    stage_own(1)
    stage_own(2)
    stage_own(0)
    meta_pass_on()
    stage_near(0)
    stage_near(1)
    build_some(64, 80)
    stage_pass(5)
    stage_pass(6)
    stage_pass(7)
    stage_near(2)
    stage_pass(0)
    build_some(80, 96)
    stage_near(3)
    stage_pass(1)
    build_some(96, 112)
    stage_far(5)
    stage_far(6)
    stage_far(7)
    build_some(112, 128)
    meta_take()
    stage_far(0)
    meta_copy.wait()

    def step(i, carry):
        for t in range(CHUNKS):
            @pl.when(i == t)
            def _():
                if t + 4 < EARLY:
                    stage_near(t + 4)
                if t + 2 < EARLY:
                    stage_pass(t + 2)
                if t + 1 < EARLY:
                    stage_far(t + 1)
                if t + 1 in late:
                    stage_late(t + 1)

        stage_product(i)
        sum_along(i)
        return carry

    lax.fori_loop(0, CHUNKS, step, 0)

    for way in range(2):
        z_next(1, way).wait_recv()
    mine = c_part[7] + z_full[1, 0] + z_full[1, 1]
    remote(c_x_out, c_x_in, h_send, h_recv, x_far).wait_recv()
    out[...] = mine + c_x_in[...]

    def sent(ref, sem):
        remote(ref, ref, sem, h_recv, x_far).wait_send()

    def some(count):
        return a_all.at[pl.ds(0, count), 0, 0]

    @pl.when(local_target)
    def _():
        sent(some(7), scat_send)
        sent(meta_in.at[pl.ds(0, 7)], meta_send)

    @pl.when(jnp.logical_not(local_target))
    def _():
        sent(some(8), scat_send)
        sent(meta_in, meta_send)

    sent(meta_v.at[core], meta_swap_send)
    sent(some(CHUNKS - LATE), x_send.at[0])
    sent(a_all.at[pl.ds(0, LATE), :, 0], x_send.at[1])
    for way in range(2):
        sent(some(CHUNKS), own_send.at[way])
        sent(some(CHUNKS - LATE), near_send.at[way])
        sent(some(CHUNKS - LATE), pass_send.at[way])
        sent(a_all.at[pl.ds(0, LATE), 0, 0, pl.ds(0, HALF)], pass_half_send.at[way])
        for e in range(2):
            z_farthest(e, way).wait_send()
            z_next(e, way).wait_send()
    sent(a_all.at[pl.ds(0, CHUNKS)], core_send)
    sent(c_x_out, h_send)


def on_device(a_blocks, a_rows, a_cols, a_keep, b_blocks, b_rows, b_cols):
    dma = pltpu.SemaphoreType.DMA
    return pl.pallas_call(
        kernel,
        out_shape=jax.ShapeDtypeStruct((RW * BS, CW * BS), F32),
        in_specs=[pl.BlockSpec(memory_space=pltpu.SMEM)] * 5 + [pl.BlockSpec(memory_space=pl.ANY)] * 2,
        out_specs=pl.BlockSpec(memory_space=pltpu.VMEM),
        scratch_shapes=[
            pltpu.VMEM((SA, BS, BS), F32),
            pltpu.VMEM((ROWS, 128), F32),
            pltpu.VMEM((16, 4, 2, PIECE, 128), F32),
            pltpu.VMEM((SB, BS, BS), F32),
            pltpu.VMEM((SB + 1, BS, 128), BF16),
            pltpu.VMEM((SB + 1, BS, 128), BF16),
            pltpu.VMEM((2 * KG, BS, CW * BS), BF16),
            pltpu.VMEM((2 * KG, BS, CW * BS), BF16),
            pltpu.VMEM((8, 128), jnp.int32),
            pltpu.VMEM((8, 8, 128), jnp.int32),
            pltpu.VMEM((2, 8, 128), jnp.int32),
            pltpu.SMEM((2, 8, 128), jnp.int32),
            pltpu.VMEM((8, 128), jnp.int32),
            pltpu.SMEM((8, 128), jnp.int32),
            pltpu.VMEM((CHUNKS, RW * BS, CW * BS), F32),
            pltpu.VMEM((2, 2, BS, CW * BS), F32),
            pltpu.VMEM((2, 2, RW * BS, CW * BS), F32),
            pltpu.VMEM((RW * BS, CW * BS), F32),
            pltpu.VMEM((RW * BS, CW * BS), F32),
            dma((2,)), dma((2,)), dma, dma((CHUNKS,)), dma, dma, dma, dma,
            dma((2,)), dma((CHUNKS,)), dma((2,)), dma((2, CHUNKS)), dma((2,)), dma((2, CHUNKS)),
            dma((2,)), dma((2,)), dma((2, CHUNKS)),
            dma, dma((CHUNKS,)), dma((2, 2)), dma((2, 2)), dma((2, 2)), dma((2, 2)), dma, dma,
        ],
        compiler_params=pltpu.CompilerParams(
            collective_id=0, has_side_effects=True, vmem_limit_bytes=56 * 1024 * 1024
        ),
        cost_estimate=pl.CostEstimate(flops=2 * 3 * 1024 * 2560 * 512, bytes_accessed=8 << 20, transcendentals=0),
    )(a_rows, a_cols, a_keep, b_rows, b_cols, a_blocks, b_blocks)


def solution(mesh):
    in_specs = (
        P(("row", "col"), None, None),
        P(("row", "col")),
        P(("row", "col")),
        P(("row", "col")),
        P(("row", "col"), None, None),
        P(("row", "col")),
        P(("row", "col")),
    )
    return jax.shard_map(
        on_device, mesh=mesh, in_specs=in_specs, out_specs=P("row", "col"), check_vma=False
    )
```

time: 68.7 us -> 58.7 us (0.85)
  Pallas kernels: 66.2 us -> 56.8 us
    pallas_call x1, Pallas kernels: 66.2 us -> 56.8 us  [on_device(): pl.pallas_call(kernel, out_shape=jax.ShapeDtypeStruct((RW * BS, CW * BS),...]
where the time goes in v2:
time: 58.7 us; the launch traced here: 58.5 us
  Pallas kernels  56.8 us (97%)
  local copies, waits for them, and re-layouts  1.67 us (3%)
    pallas_call x1, Pallas kernels, on_device(): pl.pallas_call(kernel, out_shape=jax.ShapeDtypeStruct((RW * BS, CW * BS),...  56.8 us
    unnamed x1, local copies, waits for them, and re-layouts  1.67 us

profile of v2, /device:TPU:0, one launch (start us, length us, event | category | flops | bytes accessed | tf_op | source)
XLA Modules:
  0.0 58.5 jit_solution(10563823629858415034)
XLA Ops:
  0.0 56.8 %shard_map.73 = f32[128,512]{1,0:T(8,128)} custom-call(s32[20]{0:T(128)} %a_rows.1, s32[20]{0:T(128)} %a_cols.1, s32[20]{0:T(128)} %a_keep.1, s32[64]{0:T(128)} %b_rows.1, s32[64]{0:T(128)} %b_cols.1, f32[20,64,64]{2,1,0:T(8,128)} %a_hbm.1, f32[64,64,64]{2,1,0:T(8,128)} %b_hbm.1), custom_call_target="tpu_custom_call" | custom-call | flops 8053063680 | bytes 8388608 | tf_op jit(solution)/shard_map/pallas_call | solution.py:408
  56.8 1.7 %copy.9 = f32[128,512]{1,0:T(8,128)} copy(f32[128,512]{1,0:T(8,128)} %shard_map.73) | data formatting | bytes 524288

commit v3 on v2

--- a/solution.py
+++ b/solution.py
@@ -19,8 +19,18 @@
 PIECE = ROWS // 8
 HALF = PIECE // 2
 CHUNKS = 8
-LATE = 3
-EARLY = CHUNKS - LATE
+CROSS_LAST = (4, 5, 6)
+BEFORE = (
+    (("pass", 3), ("far", 1)),
+    (("pass", 7), ("far", 2)),
+    (("far", 3),),
+    (("late", 4),),
+    (("late", 5),),
+    (("late", 6),),
+    (("far", 7),),
+    (),
+)
+LATE = len(CROSS_LAST)
 UNROLL = 2
 F32 = jnp.float32
 BF16 = jnp.bfloat16
@@ -132,16 +142,20 @@
     table_copy = pltpu.make_async_copy(table_v, table_s, smem_sem.at[0])
     table_copy.start()
 
+    def rank(t):
+        group = (t + 1) // 3
+        return t - group * (2 - group) + 3 * ((t + 6) // 7 - (t + 5) // 7)
+
     def chunk_of(t):
-        turn = t % 4
+        turn = rank(t) % 4
         away = (2 + turn + (turn // 2) * (5 - 2 * turn)) % 4
-        return (x_hi + 1 - t // 4) % 2 * 4 + (z + away) % 4
+        return (x_hi + 1 - rank(t) // 4) % 2 * 4 + (z + away) % 4
 
     def plane(t):
         return a_all.at[2 * chunk_of(t) + core]
 
     def crosses_late(t):
-        return t >= EARLY
+        return t in CROSS_LAST
 
     def own(t):
         return plane(t).at[y, x_lo]
@@ -155,7 +169,7 @@
             same(piece, x_send.at[0], x_recv.at[t], x_near).start()
 
     def stage_near(t):
-        if t < EARLY:
+        if not crosses_late(t):
             piece = plane(t).at[y, 1 - x_lo]
             same(piece, x_send.at[0], x_recv.at[t], x_near).wait_recv()
             for way in range(2):
@@ -235,7 +249,7 @@
                 total += jnp.dot(left_high, right_high, preferred_element_type=F32)
                 total += jnp.dot(left_low, right_high, preferred_element_type=F32)
                 total += jnp.dot(left_high, right_low, preferred_element_type=F32)
-        c_part[t] = total
+        c_part[rank(t)] = total
 
     def part_rows(way):
         return pl.ds(way * BS, BS)
@@ -246,33 +260,50 @@
             zh_send.at[e, way], zh_recv.at[e, way], z_way[way],
         )
 
-    def z_next(e, way):
+    def z_next(e, way, part):
         return remote(
-            c_part.at[4 * e + 2 - way], z_full.at[e, way],
-            zf_send.at[e, way], zf_recv.at[e, way], z_way[way],
+            c_part.at[4 * e + 2 - way, part_rows(part)], z_full.at[e, way, part_rows(part)],
+            zf_send.at[e, way, part], zf_recv.at[e, way, part], z_way[way],
         )
 
+    def x_last(part):
+        return remote(
+            c_x_out.at[part_rows(part)], c_x_in.at[part_rows(part)], h_send.at[part], h_recv.at[part], x_far
+        )
+
+    def pass_along(e):
+        for way in (1, 0):
+            z_farthest(e, way).wait_recv()
+            c_part[4 * e + 2 - way, part_rows(way), :] += z_half[e, way]
+            for part in range(2):
+                z_next(e, way, part).start()
+
+    def arrived(e, part):
+        for way in range(2):
+            z_next(e, way, part).wait_recv()
+        rows = part_rows(part)
+        return c_part[4 * e + 3, rows, :] + z_full[e, 0, rows, :] + z_full[e, 1, rows, :]
+
     def sum_along(t):
-        e = t // 4
-
-        @pl.when(t % 4 == 0)
-        def _():
-            for way in range(2):
-                z_farthest(e, way).start()
-
-        @pl.when(t % 4 == 2)
-        def _():
-            for way in (1, 0):
-                z_farthest(e, way).wait_recv()
-                c_part[4 * e + 2 - way, part_rows(way), :] += z_half[e, way]
-                z_next(e, way).start()
-
-        @pl.when(t == 5)
-        def _():
-            for way in range(2):
-                z_next(0, way).wait_recv()
-            c_x_out[...] = c_part[3] + z_full[0, 0] + z_full[0, 1]
-            remote(c_x_out, c_x_in, h_send, h_recv, x_far).start()
+        for e in range(2):
+            @pl.when(t == e)
+            def _():
+                for way in range(2):
+                    z_farthest(e, way).start()
+
+        @pl.when(t == 3)
+        def _():
+            pass_along(0)
+
+        @pl.when(t == 6)
+        def _():
+            pass_along(1)
+
+        @pl.when(t == 6)
+        def _():
+            for part in range(2):
+                c_x_out[part_rows(part), :] = arrived(0, part)
+                x_last(part).start()
 
     first_half = lax.broadcasted_iota(jnp.int32, (BS, 2 * BS), 1) < BS
 
@@ -303,7 +334,6 @@
     for ref in (twice_hi, twice_lo):
         ref[SB] = jnp.zeros((BS, 2 * BS), BF16)
 
-    late = range(EARLY, CHUNKS)
     def meta_pass_on():
         pltpu.make_async_copy(meta_in, meta_in, meta_recv).wait()
         for i in range(8):
@@ -318,47 +348,43 @@
 
     table_copy.wait()
     build_some(0, 64)
-    stage_own(7)
     stage_own(5)
     stage_own(6)
+    stage_own(1)
     stage_own(4)
+    stage_own(7)
+    stage_own(2)
     stage_own(3)
-    stage_own(1)
-    stage_own(2)
     stage_own(0)
     meta_pass_on()
     stage_near(0)
     stage_near(1)
     build_some(64, 80)
+    stage_pass(4)
     stage_pass(5)
     stage_pass(6)
-    stage_pass(7)
     stage_near(2)
     stage_pass(0)
     build_some(80, 96)
     stage_near(3)
     stage_pass(1)
     build_some(96, 112)
+    stage_far(4)
     stage_far(5)
     stage_far(6)
-    stage_far(7)
+    stage_near(7)
+    stage_pass(2)
     build_some(112, 128)
     meta_take()
     stage_far(0)
     meta_copy.wait()
 
     def step(i, carry):
-        for t in range(CHUNKS):
-            @pl.when(i == t)
+        for at, stages in enumerate(BEFORE):
+            @pl.when(i == at)
             def _():
-                if t + 4 < EARLY:
-                    stage_near(t + 4)
-                if t + 2 < EARLY:
-                    stage_pass(t + 2)
-                if t + 1 < EARLY:
-                    stage_far(t + 1)
-                if t + 1 in late:
-                    stage_late(t + 1)
+                for stage, t in stages:
+                    {"own": stage_own, "near": stage_near, "pass": stage_pass, "far": stage_far, "late": stage_late}[stage](t)
 
         stage_product(i)
         sum_along(i)
@@ -366,14 +392,13 @@
 
     lax.fori_loop(0, CHUNKS, step, 0)
 
-    for way in range(2):
-        z_next(1, way).wait_recv()
-    mine = c_part[7] + z_full[1, 0] + z_full[1, 1]
-    remote(c_x_out, c_x_in, h_send, h_recv, x_far).wait_recv()
-    out[...] = mine + c_x_in[...]
+    for part in range(2):
+        mine = arrived(1, part)
+        x_last(part).wait_recv()
+        out[part_rows(part), :] = mine + c_x_in[part_rows(part), :]
 
     def sent(ref, sem):
-        remote(ref, ref, sem, h_recv, x_far).wait_send()
+        remote(ref, ref, sem, load_sem.at[0], x_far).wait_send()
 
     def some(count):
         return a_all.at[pl.ds(0, count), 0, 0]
@@ -398,9 +423,11 @@
         sent(a_all.at[pl.ds(0, LATE), 0, 0, pl.ds(0, HALF)], pass_half_send.at[way])
         for e in range(2):
             z_farthest(e, way).wait_send()
-            z_next(e, way).wait_send()
+            for part in range(2):
+                z_next(e, way, part).wait_send()
     sent(a_all.at[pl.ds(0, CHUNKS)], core_send)
-    sent(c_x_out, h_send)
+    for part in range(2):
+        x_last(part).wait_send()
 
 
 def on_device(a_blocks, a_rows, a_cols, a_keep, b_blocks, b_rows, b_cols):
@@ -433,7 +460,7 @@
             dma((2,)), dma((2,)), dma, dma((CHUNKS,)), dma, dma, dma, dma,
             dma((2,)), dma((CHUNKS,)), dma((2,)), dma((2, CHUNKS)), dma((2,)), dma((2, CHUNKS)),
             dma((2,)), dma((2,)), dma((2, CHUNKS)),
-            dma, dma((CHUNKS,)), dma((2, 2)), dma((2, 2)), dma((2, 2)), dma((2, 2)), dma, dma,
+            dma, dma((CHUNKS,)), dma((2, 2)), dma((2, 2)), dma((2, 2, 2)), dma((2, 2, 2)), dma((2,)), dma((2,)),
         ],
         compiler_params=pltpu.CompilerParams(
             collective_id=0, has_side_effects=True, vmem_limit_bytes=56 * 1024 * 1024

time: 58.7 us -> 56.8 us (0.968)
  Pallas kernels: 56.8 us -> 55 us
    pallas_call x1, Pallas kernels: 56.8 us -> 55 us  [on_device(): pl.pallas_call(kernel, out_shape=jax.ShapeDtypeStruct((RW * BS, CW * BS),...]
where the time goes in v3:
time: 56.8 us; the launch traced here: 56.6 us
  Pallas kernels  55 us (97%)
  local copies, waits for them, and re-layouts  1.67 us (3%)
    pallas_call x1, Pallas kernels, on_device(): pl.pallas_call(kernel, out_shape=jax.ShapeDtypeStruct((RW * BS, CW * BS),...  55 us
    unnamed x1, local copies, waits for them, and re-layouts  1.67 us

profile of v3, /device:TPU:0, one launch (start us, length us, event | category | flops | bytes accessed | tf_op | source)
XLA Modules:
  0.0 56.6 jit_solution(8379650160550526292)
XLA Ops:
  0.0 55.0 %shard_map.73 = f32[128,512]{1,0:T(8,128)} custom-call(s32[20]{0:T(128)} %a_rows.1, s32[20]{0:T(128)} %a_cols.1, s32[20]{0:T(128)} %a_keep.1, s32[64]{0:T(128)} %b_rows.1, s32[64]{0:T(128)} %b_cols.1, f32[20,64,64]{2,1,0:T(8,128)} %a_hbm.1, f32[64,64,64]{2,1,0:T(8,128)} %b_hbm.1), custom_call_target="tpu_custom_call" | custom-call | flops 8053063680 | bytes 8388608 | tf_op jit(solution)/shard_map/pallas_call | solution.py:435
  55.0 1.7 %copy.9 = f32[128,512]{1,0:T(8,128)} copy(f32[128,512]{1,0:T(8,128)} %shard_map.73) | data formatting | bytes 524288

commit v4 on v3

--- a/solution.py
+++ b/solution.py
@@ -81,6 +81,45 @@
     load_a.start()
     load_b.start()
 
+    load_a.wait()
+    for p in range(PAIRS):
+        packed[pl.ds(p * BS, BS), :] = jnp.concatenate([a_raw[2 * p], a_raw[2 * p + 1]], axis=1)
+
+    @pl.when(local_target)
+    def _():
+        pl.semaphore_wait(barrier, 14)
+
+    @pl.when(jnp.logical_not(local_target))
+    def _():
+        pl.semaphore_wait(barrier, 15)
+
+    run = r * 2 + half
+
+    def remote(src, dst, send, recv, peer):
+        return pltpu.make_async_remote_copy(src, dst, send, recv, device_id=peer, device_id_type=MESH)
+
+    def same(ref, send, recv, peer):
+        return remote(ref, ref, send, recv, peer)
+
+    def scatter(step, carry):
+        p = (step + 2 * z + 4 * x_hi + y) % 8
+        target = (kappa, (p // 2) * 4 + (p % 2) * 2 + half)
+        piece = packed.at[pl.ds(pl.multiple_of(p * PIECE, 16), PIECE)]
+        place = a_all.at[run, p // 2, p % 2]
+        here = jnp.logical_and(target[0] == r, target[1] == c)
+
+        @pl.when(here)
+        def _():
+            pltpu.make_async_copy(piece, place, scat_recv.at[r]).start()
+
+        @pl.when(jnp.logical_not(here))
+        def _():
+            remote(piece, place, scat_send, scat_recv.at[r], target).start()
+
+        return carry
+
+    lax.fori_loop(0, 8, scatter, 0)
+
     lane = lax.broadcasted_iota(jnp.int32, (8, 128), 1)
     sub = lax.broadcasted_iota(jnp.int32, (8, 128), 0)
     meta = jnp.zeros((8, 128), jnp.int32)
@@ -92,45 +131,21 @@
         meta = jnp.where(lane == 64 + a, keep * low_row, meta)
     meta_out[...] = meta
 
-    load_a.wait()
-    for p in range(PAIRS):
-        packed[pl.ds(p * BS, BS), :] = jnp.concatenate([a_raw[2 * p], a_raw[2 * p + 1]], axis=1)
-
-    @pl.when(local_target)
-    def _():
-        pl.semaphore_wait(barrier, 14)
-
-    @pl.when(jnp.logical_not(local_target))
-    def _():
-        pl.semaphore_wait(barrier, 15)
-
-    run = r * 2 + half
-
-    def remote(src, dst, send, recv, peer):
-        return pltpu.make_async_remote_copy(src, dst, send, recv, device_id=peer, device_id_type=MESH)
-
-    def same(ref, send, recv, peer):
-        return remote(ref, ref, send, recv, peer)
-
-    def scatter(p, carry):
+    def tell(p, carry):
         target = (kappa, (p // 2) * 4 + (p % 2) * 2 + half)
-        piece = packed.at[pl.ds(pl.multiple_of(p * PIECE, 16), PIECE)]
-        place = a_all.at[run, p // 2, p % 2]
         here = jnp.logical_and(target[0] == r, target[1] == c)
 
         @pl.when(here)
         def _():
-            pltpu.make_async_copy(piece, place, scat_recv.at[r]).start()
             pltpu.make_async_copy(meta_out, meta_in.at[r], meta_recv).start()
 
         @pl.when(jnp.logical_not(here))
         def _():
-            remote(piece, place, scat_send, scat_recv.at[r], target).start()
             remote(meta_out, meta_in.at[r], meta_send, meta_recv, target).start()
 
         return carry
 
-    lax.fori_loop(0, 8, scatter, 0)
+    lax.fori_loop(0, 8, tell, 0)
 
     flat = sub * 128 + lane
     table = jnp.full((8, 128), SB, jnp.int32)
@@ -275,7 +290,7 @@
         for way in (1, 0):
             z_farthest(e, way).wait_recv()
             c_part[4 * e + 2 - way, part_rows(way), :] += z_half[e, way]
-            for part in range(2):
+            for part in ((way,) if e in (1,) else range(2)):
                 z_next(e, way, part).start()
 
     def arrived(e, part):
@@ -290,6 +305,11 @@
             def _():
                 for way in range(2):
                     z_farthest(e, way).start()
+
+        for e, way, turn in ((1, 1, 5), (1, 0, 6), ):
+            @pl.when(t == turn)
+            def _():
+                z_next(e, way, 1 - way).start()
 
         @pl.when(t == 3)
         def _():
@@ -359,19 +379,19 @@
     meta_pass_on()
     stage_near(0)
     stage_near(1)
-    build_some(64, 80)
     stage_pass(4)
     stage_pass(5)
     stage_pass(6)
+    build_some(64, 80)
     stage_near(2)
     stage_pass(0)
     build_some(80, 96)
     stage_near(3)
     stage_pass(1)
-    build_some(96, 112)
     stage_far(4)
     stage_far(5)
     stage_far(6)
+    build_some(96, 112)
     stage_near(7)
     stage_pass(2)
     build_some(112, 128)

time: 56.8 us -> 56 us (0.986)
  Pallas kernels: 55 us -> 54.1 us
    pallas_call x1, Pallas kernels: 55 us -> 54.1 us  [on_device(): pl.pallas_call(kernel, out_shape=jax.ShapeDtypeStruct((RW * BS, CW * BS),...]
where the time goes in v4:
time: 56 us; the launch traced here: 55.8 us
  Pallas kernels  54.1 us (97%)
  local copies, waits for them, and re-layouts  1.67 us (3%)
    pallas_call x1, Pallas kernels, on_device(): pl.pallas_call(kernel, out_shape=jax.ShapeDtypeStruct((RW * BS, CW * BS),...  54.1 us
    unnamed x1, local copies, waits for them, and re-layouts  1.67 us

profile of v4, /device:TPU:0, one launch (start us, length us, event | category | flops | bytes accessed | tf_op | source)
XLA Modules:
  0.0 55.8 jit_solution(7273761032745574048)
XLA Ops:
  0.0 54.1 %shard_map.73 = f32[128,512]{1,0:T(8,128)} custom-call(s32[20]{0:T(128)} %a_rows.1, s32[20]{0:T(128)} %a_cols.1, s32[20]{0:T(128)} %a_keep.1, s32[64]{0:T(128)} %b_rows.1, s32[64]{0:T(128)} %b_cols.1, f32[20,64,64]{2,1,0:T(8,128)} %a_hbm.1, f32[64,64,64]{2,1,0:T(8,128)} %b_hbm.1), custom_call_target="tpu_custom_call" | custom-call | flops 8053063680 | bytes 8388608 | tf_op jit(solution)/shard_map/pallas_call | solution.py:455
  54.1 1.7 %copy.9 = f32[128,512]{1,0:T(8,128)} copy(f32[128,512]{1,0:T(8,128)} %shard_map.73) | data formatting | bytes 524288

commit v5 on v4

--- a/solution.py
+++ b/solution.py
@@ -367,31 +367,33 @@
         meta_copy.start()
 
     table_copy.wait()
-    build_some(0, 64)
+    build_some(0, 32)
     stage_own(5)
     stage_own(6)
     stage_own(1)
+    build_some(32, 48)
     stage_own(4)
     stage_own(7)
+    build_some(48, 64)
     stage_own(2)
     stage_own(3)
     stage_own(0)
     meta_pass_on()
     stage_near(0)
     stage_near(1)
+    build_some(64, 80)
     stage_pass(4)
     stage_pass(5)
     stage_pass(6)
-    build_some(64, 80)
     stage_near(2)
     stage_pass(0)
     build_some(80, 96)
     stage_near(3)
     stage_pass(1)
+    build_some(96, 112)
     stage_far(4)
     stage_far(5)
     stage_far(6)
-    build_some(96, 112)
     stage_near(7)
     stage_pass(2)
     build_some(112, 128)

time: 56 us -> 55.8 us (level)
  no operation moved by 1% of the time
where the time goes in v5:
time: 55.8 us; the launch traced here: 55.6 us
  Pallas kernels  53.9 us (97%)
  local copies, waits for them, and re-layouts  1.67 us (3%)
    pallas_call x1, Pallas kernels, on_device(): pl.pallas_call(kernel, out_shape=jax.ShapeDtypeStruct((RW * BS, CW * BS),...  53.9 us
    unnamed x1, local copies, waits for them, and re-layouts  1.67 us

profile of v5, /device:TPU:0, one launch (start us, length us, event | category | flops | bytes accessed | tf_op | source)
XLA Modules:
  0.0 55.6 jit_solution(2625928177795090636)
XLA Ops:
  0.0 53.9 %shard_map.73 = f32[128,512]{1,0:T(8,128)} custom-call(s32[20]{0:T(128)} %a_rows.1, s32[20]{0:T(128)} %a_cols.1, s32[20]{0:T(128)} %a_keep.1, s32[64]{0:T(128)} %b_rows.1, s32[64]{0:T(128)} %b_cols.1, f32[20,64,64]{2,1,0:T(8,128)} %a_hbm.1, f32[64,64,64]{2,1,0:T(8,128)} %b_hbm.1), custom_call_target="tpu_custom_call" | custom-call | flops 8053063680 | bytes 8388608 | tf_op jit(solution)/shard_map/pallas_call | solution.py:457
  53.9 1.7 %copy.9 = f32[128,512]{1,0:T(8,128)} copy(f32[128,512]{1,0:T(8,128)} %shard_map.73) | data formatting | bytes 524288
